TPU v7x, 256 devices: a whole 4x4x8 slice. The times are simulated.
256 devices in a mesh: dp: 32 (over y_lo, z, core), tensor: 8 (over y_hi, x).
Axes of the slice: x: 4, y: 4 (y_hi: 2, y_lo: 2; y = y_hi * 2 + y_lo), z: 8, core: 2. Of those that a mesh axis runs over, the one named last changes fastest.
Arguments:
- image_features: bfloat16 [8192, 1408], P('dp', 'tensor'), may hold values from -6 to 6
- text_features: bfloat16 [8192, 1152], P('dp', 'tensor'), may hold values from -6 to 6
- image_weight: bfloat16 [1408, 1152], P('tensor'), may hold values from -0.15625 to 0.15625
- text_weight: bfloat16 [1152, 1152], P('tensor'), may hold values from -0.1875 to 0.1875
- image_pair: int32 [8192], P('dp'), may hold values from 0 to 8191, each once
- temp_index: int32 [], replicated, may hold values from 0 to 8
- bias_index: int32 [], replicated, may hold values from 2 to 7
Outputs:
- grad_image_weight: float32 [1408, 1152], P('tensor', 'dp')
- grad_text_weight: float32 [1152, 1152], P('tensor', 'dp')
Inputs may be any that keep to these rules, and one draw needn't show every extreme that they name: image_pair holds each text row index exactly once.
All inputs are finite; a program needn't handle non-finite values.
Results may differ from a plain program's by a relative error of at most 0.0034.
Values may be sent and summed in bfloat16 or wider, within the bound.
A program may use at most 64 MiB of HBM per device.

v0:
```python
import jax
import jax.numpy as jnp
from jax import lax
from jax.sharding import PartitionSpec as P


def unit_rows(values):
    norm = jnp.sqrt(jnp.sum(values * values, axis=1, keepdims=True) + 1e-06)
    direct = values / norm
    return (norm, direct)


def back_rows(direct, norm, grad):
    inner = jnp.sum(direct * grad, axis=1, keepdims=True)
    return ((grad - direct * inner) / norm).astype(jnp.bfloat16)


def pair_weights(img_unit, txt_block, col_index, targets, scale, shift):
    logits = scale * jnp.dot(img_unit, txt_block.T, preferred_element_type=jnp.float32) + shift
    sign = jnp.where(col_index[None, :] == targets[:, None], jnp.float32(1.0), jnp.float32(-1.0))
    return (-scale * sign * jax.nn.sigmoid(-sign * logits)).astype(jnp.bfloat16)


def on_device(
    image_features, text_features, image_weight, text_weight, image_pair, temp_index, bias_index
):
    scale = 4.0 + temp_index.astype(jnp.float32)
    shift = -0.5 * bias_index.astype(jnp.float32)
    rows = image_features.shape[0]
    groups = lax.axis_size("tensor")
    pieces = rows // groups
    blocks = lax.axis_size("dp")
    tpos = lax.axis_index("tensor")
    contract = (((0,), (0,)), ((), ()))
    img_part = jnp.dot(image_features, image_weight, preferred_element_type=jnp.float32)
    txt_part = jnp.dot(text_features, text_weight, preferred_element_type=jnp.float32)
    img = lax.psum(img_part, "tensor")
    txt = lax.psum_scatter(txt_part, "tensor", scatter_dimension=0, tiled=True)
    img_norm, img_dir = unit_rows(img)
    txt_norm, txt_dir = unit_rows(txt)
    img_unit = img_dir.astype(jnp.bfloat16)
    txt_unit = txt_dir.astype(jnp.bfloat16)
    gathered = lax.all_gather(txt_unit, "dp", axis=0, tiled=True)
    flat = jnp.arange(blocks * pieces, dtype=jnp.int32)
    col_index = flat // pieces * rows + tpos * pieces + flat % pieces
    weights = pair_weights(img_unit, gathered, col_index, image_pair, scale, shift)
    img_grad_part = jnp.dot(weights, gathered, preferred_element_type=jnp.float32)
    txt_grad_unit = lax.psum_scatter(
        lax.dot_general(weights, img_unit, contract, preferred_element_type=jnp.float32),
        "dp",
        scatter_dimension=0,
        tiled=True,
    )
    img_grad_unit = lax.psum(img_grad_part, "tensor")
    img_grad = back_rows(img_dir, img_norm, img_grad_unit)
    txt_grad_piece = back_rows(txt_dir, txt_norm, txt_grad_unit)
    txt_grad = lax.all_gather(txt_grad_piece, "tensor", axis=0, tiled=True)
    image_term = lax.dot_general(
        image_features, img_grad, contract, preferred_element_type=jnp.float32
    )
    text_term_all = lax.dot_general(
        text_features, txt_grad, contract, preferred_element_type=jnp.float32
    )
    grad_image_weight, grad_text_weight = (
        lax.psum_scatter(image_term, "dp", scatter_dimension=1, tiled=True),
        lax.psum_scatter(text_term_all, "dp", scatter_dimension=1, tiled=True),
    )
    return (grad_image_weight, grad_text_weight)


def solution(mesh):
    return jax.shard_map(
        on_device,
        mesh=mesh,
        in_specs=(
            P("dp", "tensor"),
            P("dp", "tensor"),
            P("tensor", None),
            P("tensor", None),
            P("dp"),
            P(),
            P(),
        ),
        out_specs=(P("tensor", "dp"), P("tensor", "dp")),
        check_vma=False,
    )
```

profile of v0, /device:TPU:1, one launch (start us, length us, event | category | flops | bytes accessed | tf_op | source)
XLA Modules:
  0.0 745.2 jit_solution(1691465190071701374)
XLA Ops:
  7.2 0.0 reduce-scatter.5.cloned.1.call-start
  7.2 2.5 fusion.23
  9.7 0.0 reduce-scatter.5.cloned.1.call-update
  9.7 0.0 all-reduce.7.cloned.1.call-start
  9.8 1.4 fusion.22
  11.2 0.0 all-gather.2.cloned.1.call-start
  11.3 81.2 %reduce-scatter.5.cloned.1.call-done = f32[32,1152]{1,0:T(8,128)} async-done(((f32[256,1152]{1,0:T(8,128)}), f32[32,1152]{1,0:T(8,128)}) %reduce-scatter.5.cloned.1.call-update) | async-done | bytes 147472 | tf_op jit(solution)/shard_map/reduce_scatter | solution.py:38
  92.5 1.0 multiply_reduce_fusion.3
  93.5 1.6 fusion.21
  95.2 0.0 all-reduce.9.cloned.1.call-start
  96.5 88.1 %all-reduce.7.cloned.1.call-done = f32[256,1152]{1,0:T(8,128)} async-done(((f32[256,1152]{1,0:T(8,128)}), f32[256,1152]{1,0:T(8,128)}) %all-reduce.7.cloned.1.call-update) | async-done | bytes 1179664 | tf_op jit(solution)/shard_map/psum | solution.py:37
  184.7 1.5 multiply_reduce_fusion.1
  186.2 69.2 %all-gather.2.cloned.1.call-done = bf16[1024,1152]{1,0:T(8,128)(2,1)} async-done(((bf16[32,1152]{1,0:T(8,128)(2,1)}), bf16[1024,1152]{1,0:T(8,128)(2,1)}) %all-gather.2.cloned.1.call-update) | async-done | bytes 2359312 | tf_op jit(solution)/shard_map/all_gather | solution.py:43
  255.4 2.9 fusion.7
  258.4 1.9 fusion.24
  260.3 0.0 reduce-scatter.7.cloned.1.call-start
  260.3 3.1 fusion.8
  263.4 0.0 all-reduce.11.cloned.1.call-start
  263.4 84.9 %all-reduce.9.cloned.1.call-done = f32[256,1152]{1,0:T(8,128)} async-done(((f32[256,1152]{1,0:T(8,128)}), f32[256,1152]{1,0:T(8,128)}) %all-reduce.9.cloned.1.call-update) | async-done | bytes 1179664 | tf_op jit(solution)/shard_map/psum | solution.py:54
  348.3 1.7 multiply_reduce_fusion
  350.0 1.4 convolution_bitcast_fusion
  351.4 121.7 %reduce-scatter.7.cloned.1.call-done = f32[32,1152]{1,0:T(8,128)} async-done(((f32[1024,1152]{1,0:T(8,128)}), f32[32,1152]{1,0:T(8,128)}) %reduce-scatter.7.cloned.1.call-update) | async-done | bytes 147472 | tf_op jit(solution)/shard_map/reduce_scatter | solution.py:48
  473.1 1.1 multiply_reduce_fusion.2
  474.2 1.0 divide_convert_fusion.2
  475.2 29.6 %all_gather.7 = bf16[256,1152]{1,0:T(8,128)(2,1)S(1)} all-gather(bf16[32,1152]{1,0:T(8,128)(2,1)S(1)} %divide_convert_fusion.2), channel_id=1, replica_groups=mesh['dp'=32,'tensor'=8] {'tensor'}, dimensions={0}, use_global_device_ids=true | all-gather | bytes 663552 | tf_op jit(solution)/shard_map/all_gather | solution.py:57
  504.8 1.1 convolution_bitcast_fusion.1
  505.9 0.6 dynamic-slice
  507.2 227.7 %all-reduce.11.cloned.1.call-done = (f32[176,1152]{1,0:T(8,128)}, f32[144,1152]{1,0:T(8,128)}) async-done(((f32[176,1152]{1,0:T(8,128)}, f32[144,1152]{1,0:T(8,128)}), (f32[176,1152]{1,0:T(8,128)}, f32[144,1152]{1,0:T(8,128)})) %all-reduce.11.cloned.1.call-update) | async-done | bytes 1474576
  734.9 1.0 constant_dynamic-slice_fusion.1
  735.9 0.7 copy.11
  736.6 1.0 constant_dynamic-slice_fusion
  737.6 0.7 copy.12
  (26 shorter events, 0.1 us)
Async XLA Ops:
  7.2 2.6 copy-start
  7.2 2.6 copy-start.6
  7.2 85.3 %reduce-scatter.5.cloned.1.call-start = ((), (), s32[]{:S(2)}) async-start(), calls=%async_computation.3 | async-start | bytes 1327104 | tf_op jit(solution)/shard_map/reduce_scatter | solution.py:38
  9.7 175.0 %all-reduce.7.cloned.1.call-start = ((), (), s32[]{:S(2)}) async-start(), calls=%async_computation.2 | async-start | bytes 2359296 | tf_op jit(solution)/shard_map/psum | solution.py:37
  11.2 244.2 %copy-start.7 = (s32[256]{0:T(256)S(1)}, s32[256]{0:T(256)}, u32[]{:S(2)}) copy-start(s32[256]{0:T(256)} %param.11) | copy-start | bytes 3076
  11.2 244.2 %all-gather.2.cloned.1.call-start = ((), (), s32[]{:S(2)}) async-start(), calls=%async_computation.4 | async-start | bytes 2433024 | tf_op jit(solution)/shard_map/all_gather | solution.py:43
  95.2 253.2 %all-reduce.9.cloned.1.call-start = ((), (), s32[]{:S(2)}) async-start(), calls=%async_computation.5 | async-start | bytes 2359296 | tf_op jit(solution)/shard_map/psum | solution.py:54
  184.7 70.7 %copy-start.1 = (f32[256,1152]{1,0:T(8,128)S(1)}, f32[256,1152]{1,0:T(8,128)}, u32[]{:S(2)}) copy-start(f32[256,1152]{1,0:T(8,128)} %all-reduce.7.cloned.1.call-done) | copy-start | bytes 3538948
  255.4 2.9 copy-start.2
  260.3 212.8 %reduce-scatter.7.cloned.1.call-start = ((), (), s32[]{:S(2)}) async-start(), calls=%async_computation.6 | async-start | bytes 4866048 | tf_op jit(solution)/shard_map/reduce_scatter | solution.py:48
  263.4 471.5 %all-reduce.11.cloned.1.call-start = ((), (), s32[]{:S(2)}) async-start(), calls=%async_computation.7 | async-start | bytes 2949120
  348.3 1.7 copy-start.4
  350.0 123.1 %copy-start.3 = (f32[32,1152]{1,0:T(8,128)S(1)}, f32[32,1152]{1,0:T(8,128)}, u32[]{:S(2)}) copy-start(f32[32,1152]{1,0:T(8,128)} %reduce-scatter.5.cloned.1.call-done) | copy-start | bytes 442372
  351.4 153.4 %copy-start.5 = (bf16[256,144]{0,1:T(8,128)(2,1)S(1)}, bf16[256,144]{0,1:T(8,128)(2,1)}, u32[]{:S(2)}) copy-start(bf16[256,144]{0,1:T(8,128)(2,1)} %param.8) | copy-start | bytes 221188
  504.8 1.1 copy-start.8
Sparse Core Ops, SparseCore 0:
  12.0 80.4 reduce-scatter.4
  95.3 89.3 all-reduce.6
  186.7 68.6 all-gather.1
  260.4 87.8 all-reduce.8
  350.9 122.1 reduce-scatter.6
  506.0 228.8 all-reduce.10
where the time goes:
time: 746 us; the launch traced here: 745 us
  waiting for transfers between devices  673 us (90%)
  blocking collectives  29.6 us (4%)
  between operations  16.2 us (2%)
  matrix products  14.2 us (2%)
  other arithmetic  7.99 us (1%)
    unnamed x7, waiting for transfers between devices  228 us
    reduce_scatter x1, waiting for transfers between devices, on_device(): lax.psum_scatter(lax.dot_general(weights, img_unit, contract, preferred_e...  122 us
    psum x1, waiting for transfers between devices, on_device(): img = lax.psum(img_part, 'tensor')  88.1 us
    psum x1, waiting for transfers between devices, on_device(): img_grad_unit = lax.psum(img_grad_part, 'tensor')  84.9 us
    reduce_scatter x1, waiting for transfers between devices, on_device(): txt = lax.psum_scatter(txt_part, 'tensor', scatter_dimension=0, tiled=True)  81.2 us
    all_gather x1, waiting for transfers between devices, on_device(): gathered = lax.all_gather(txt_unit, 'dp', axis=0, tiled=True)  69.2 us
    all_gather x1, blocking collectives, on_device(): txt_grad = lax.all_gather(txt_grad_piece, 'tensor', axis=0, tiled=True)  29.6 us
  transfers between devices with their start and end apart: 6, of which 6 were waited for; matrix products, arithmetic and copies ran while one was open for 2% of the time, Pallas kernels for 0%

commit v1 on v0

v1 whole, which is shorter than its diff:
```python
import functools

import jax
import jax.numpy as jnp
from jax import lax
from jax.experimental import pallas as pl
from jax.experimental.pallas import tpu as pltpu
from jax.sharding import PartitionSpec as P

MESH = pl.DeviceIdType.MESH
E = 1152
DI = 176
DT = 144
R = 32
TS = 8
ZS = 8
PS = 16
OUT = 36
OUT_ROWS = 48
OUT_LANES = 384
LEVELS = 32000.0
WIRE = E + 128
f32 = jnp.float32
bf16 = jnp.bfloat16


def encode(x, wire, k):
    m = jnp.max(jnp.abs(x), axis=1, keepdims=True)
    hi = jnp.floor(m)
    lo = jnp.floor((m - hi) * LEVELS) + 1.0
    top = hi + lo * (1.0 / LEVELS)
    wire[k, :, 0:E] = jnp.round(x * (LEVELS / top)).astype(jnp.int32).astype(jnp.int16)
    lane = lax.broadcasted_iota(jnp.int32, (R, 128), 1)
    wire[k, :, E:WIRE] = jnp.where(lane < 64, hi, lo).astype(jnp.int32).astype(jnp.int16)


def decode(wire, k):
    code = wire[k, :, E:WIRE].astype(jnp.int32).astype(f32)
    lane = lax.broadcasted_iota(jnp.int32, (R, 128), 1)
    top = jnp.sum(jnp.where(lane < 64, code, code * (1.0 / LEVELS)), axis=1, keepdims=True) * (1.0 / 64)
    return wire[k, :, 0:E].astype(jnp.int32).astype(f32) * (top * (1.0 / LEVELS))


def unit_rows(values):
    norm = jnp.sqrt(jnp.sum(values * values, axis=1, keepdims=True) + 1e-06)
    return norm, values / norm


def back_rows(direct, norm, grad):
    inner = jnp.sum(direct * grad, axis=1, keepdims=True)
    return ((grad - direct * inner) / norm).astype(bf16)


def kernel(
    temp_ref, bias_ref, pair_ref, fi_ref, ft_ref, wi_ref, wt_ref, out_ref,
    part_i, part_t, a_i_out, a_i_in, a_t_out, a_t_in,
    dir_i, dir_t, norm_i, norm_t, all_i, all_t, pair_out, pair_in,
    w_ref, gi, gt, gt_sib, gt_own, c_i_out, c_i_in, c_t_out, c_t_in,
    grad_i, grad_t, g_ref, g_sib, e_own, e_out, e_in,
    a_i_ss, a_i_rs, a_t_ss, a_t_rs, b_i_ss, b_i_rs, b_t_ss, b_t_rs, relay_ss, relay_rs,
    c_i_ss, c_i_rs, c_t_ss, c_t_rs, d_i_ss, d_i_rs, d_t_ss, d_t_rs, e_ss, e_rs, one_ss, one_rs,
):
    dp = lax.axis_index("dp")
    t = lax.axis_index("tensor")
    ylo = lax.div(dp, 16)
    z = lax.rem(lax.div(dp, 2), 8)
    c = lax.rem(dp, 2)
    oc = 1 - c
    p = ylo * TS + t
    q = ylo * ZS + z

    def device(ylo_, z_, c_, t_):
        return ((ylo_ * ZS + z_) * 2 + c_, t_)

    sibling = device(ylo, z, oc, t)
    across = device(1 - ylo, z, c, t)

    def plane(k):
        return device(lax.div(k, TS), z, c, lax.rem(k, TS))

    def column(k):
        return device(lax.div(k, ZS), lax.rem(k, ZS), c, t)

    def copy(src, dst, ssem, rsem, dev):
        return pltpu.make_async_remote_copy(
            src_ref=src, dst_ref=dst, send_sem=ssem, recv_sem=rsem, device_id=dev, device_id_type=MESH
        )

    barrier = pltpu.get_barrier_semaphore()

    def greet_plane(k, _):
        pl.semaphore_signal(barrier, inc=1, device_id=plane(lax.rem(p + k, PS)), device_id_type=MESH)
        return 0

    def greet_column(k, _):
        zz = lax.rem(z + k, ZS)
        pl.semaphore_signal(barrier, inc=1, device_id=device(ylo, zz, c, t), device_id_type=MESH)
        pl.semaphore_signal(barrier, inc=1, device_id=device(1 - ylo, zz, c, t), device_id_type=MESH)
        return 0

    lax.fori_loop(1, PS, greet_plane, 0)
    lax.fori_loop(1, ZS, greet_column, 0)
    pl.semaphore_signal(barrier, inc=1, device_id=sibling, device_id_type=MESH)

    part_t[...] = jnp.dot(ft_ref[...], wt_ref[...], preferred_element_type=f32).reshape(TS, R, E)
    pair_out[...] = jnp.broadcast_to(pair_ref[...], (8, 256))
    g_ref[...] = jnp.zeros_like(g_ref)
    pl.semaphore_wait(barrier, (PS - 1) + 2 * (ZS - 1) + 1)
    pair_copy = copy(pair_out, pair_in, one_ss.at[0], one_rs.at[0], across)
    pair_copy.start()

    def a_copy(wire_out, wire_in, ss, rs, k, slot):
        return copy(wire_out.at[k], wire_in.at[slot], ss.at[k], rs.at[slot], (dp, k))

    def a_send(part, wire_out, wire_in, ss, rs):
        def step(j, _):
            k = lax.rem(t + j, TS)
            encode(part[k], wire_out, k)
            a_copy(wire_out, wire_in, ss, rs, k, t).start()
            return 0
        lax.fori_loop(1, TS, step, 0)

    def a_take(part, wire_out, wire_in, ss, rs):
        def step(j, total):
            k = lax.rem(t + j, TS)
            a_copy(wire_out, wire_in, ss, rs, k, k).wait_recv()
            return total + decode(wire_in, k)
        return lax.fori_loop(1, TS, step, part[t])

    a_send(part_t, a_t_out, a_t_in, a_t_ss, a_t_rs)
    part_i[...] = jnp.dot(fi_ref[...], wi_ref[...], preferred_element_type=f32).reshape(TS, R, E)
    a_send(part_i, a_i_out, a_i_in, a_i_ss, a_i_rs)

    def b_t_copy(zz, slot):
        s = c * ZS + slot
        return copy(all_t.at[s], all_t.at[s], b_t_ss.at[zz], b_t_rs.at[slot], device(ylo, zz, c, t))

    def relay(cc, zz):
        s = cc * ZS + zz
        return copy(all_t.at[s], all_t.at[s], relay_ss.at[zz], relay_rs.at[zz], sibling)

    norm, direct = unit_rows(a_take(part_t, a_t_out, a_t_in, a_t_ss, a_t_rs))
    norm_t[...] = norm
    dir_t[...] = direct
    all_t[c * ZS + z] = direct.astype(bf16)

    def b_t_send(j, _):
        b_t_copy(lax.rem(z + j, ZS), z).start()
        return 0

    lax.fori_loop(1, ZS, b_t_send, 0)
    relay(c, z).start()

    def b_i_copy(k, slot):
        return copy(all_i.at[slot], all_i.at[slot], b_i_ss.at[k], b_i_rs.at[slot], plane(k))

    norm, direct = unit_rows(a_take(part_i, a_i_out, a_i_in, a_i_ss, a_i_rs))
    norm_i[...] = norm
    dir_i[...] = direct
    all_i[p] = direct.astype(bf16)

    def b_i_send(j, _):
        b_i_copy(lax.rem(p + j, PS), p).start()
        return 0

    lax.fori_loop(1, PS, b_i_send, 0)

    def b_t_take(j, _):
        zz = lax.rem(z + j, ZS)
        b_t_copy(zz, zz).wait_recv()
        relay(c, zz).start()
        return 0

    lax.fori_loop(1, ZS, b_t_take, 0)

    def b_i_take(j, _):
        k = lax.rem(p + j, PS)
        b_i_copy(k, k).wait_recv()
        return 0

    lax.fori_loop(1, PS, b_i_take, 0)

    def relay_take(zz, _):
        relay(oc, zz).wait_recv()
        return 0

    lax.fori_loop(0, ZS, relay_take, 0)
    pair_copy.wait_recv()

    scale = 4.0 + temp_ref[0].astype(f32)
    shift = -0.5 * bias_ref[0].astype(f32)

    def local_target(pair):
        r = pair & 31
        tt = (pair >> 5) & 7
        cc = (pair >> 8) & 1
        zz = (pair >> 9) & 7
        yy = (pair >> 12) & 1
        here = jnp.logical_and(tt == t, yy == ylo)
        return jnp.where(here, (cc * ZS + zz) * R + r, -1)

    own = local_target(pair_out[0:1, :])
    other = local_target(pair_in[0:1, :])
    first = jnp.where(ylo == 0, own, other)
    second = jnp.where(ylo == 0, other, own)
    target = jnp.concatenate([first, second], axis=1)

    def tile(j, _):
        b = lax.rem(2 * oc + j, 4)
        rows = all_t[pl.ds(b * 4, 4)].reshape(4 * R, E)
        img = all_i[...].reshape(PS * R, E)
        logits = scale * lax.dot_general(rows, img, (((1,), (1,)), ((), ())), preferred_element_type=f32) + shift
        index = lax.broadcasted_iota(jnp.int32, (4 * R, PS * R), 0) + b * (4 * R)
        sign = jnp.where(index == target, f32(1.0), f32(-1.0))
        w = (-scale * sign * jax.nn.sigmoid(-sign * logits)).astype(bf16)
        w_ref[pl.ds(pl.multiple_of(b * (4 * R), 4 * R), 4 * R), :] = w
        gt[pl.ds(b * 4, 4)] = jnp.dot(w, img, preferred_element_type=f32).reshape(4, R, E)
        return 0

    lax.fori_loop(0, 2, tile, 0)
    sib_copy = copy(gt.at[pl.ds(oc * ZS, ZS)], gt_sib, one_ss.at[1], one_rs.at[1], sibling)
    sib_copy.start()
    lax.fori_loop(2, 4, tile, 0)
    sib_copy.wait_recv()

    def c_t_copy(zz, slot):
        return copy(c_t_out.at[zz], c_t_in.at[slot], c_t_ss.at[zz], c_t_rs.at[slot], device(ylo, zz, c, t))

    def c_t_send(j, _):
        zz = lax.rem(z + j, ZS)
        encode(gt[c * ZS + zz] + gt_sib[zz], c_t_out, zz)
        c_t_copy(zz, z).start()
        return 0

    lax.fori_loop(1, ZS, c_t_send, 0)

    def c_i_copy(k, slot):
        return copy(c_i_out.at[k], c_i_in.at[slot], c_i_ss.at[k], c_i_rs.at[slot], plane(k))

    for b in range(4):
        gi[4 * b:4 * b + 4] = lax.dot_general(
            w_ref[:, 4 * R * b:4 * R * (b + 1)], all_t[...].reshape(PS * R, E), (((0,), (0,)), ((), ())),
            preferred_element_type=f32,
        ).reshape(4, R, E)

    def c_i_send(j, _):
        k = lax.rem(p + j, PS)
        encode(gi[k], c_i_out, k)
        c_i_copy(k, p).start()
        return 0

    lax.fori_loop(1, PS, c_i_send, 0)

    def c_i_take(j, total):
        k = lax.rem(p + j, PS)
        c_i_copy(k, k).wait_recv()
        return total + decode(c_i_in, k)

    def c_t_take(j, total):
        zz = lax.rem(z + j, ZS)
        c_t_copy(zz, zz).wait_recv()
        return total + decode(c_t_in, zz)

    def d_copy(grad, ss, rs, k, slot):
        return copy(grad.at[slot], grad.at[slot], ss.at[k], rs.at[slot], (dp, k))

    def d_send(grad, ss, rs):
        def step(j, _):
            d_copy(grad, ss, rs, lax.rem(t + j, TS), t).start()
            return 0
        lax.fori_loop(1, TS, step, 0)

    def d_take(grad, ss, rs):
        def step(j, _):
            k = lax.rem(t + j, TS)
            d_copy(grad, ss, rs, k, k).wait_recv()
            return 0
        lax.fori_loop(1, TS, step, 0)

    total = lax.fori_loop(1, ZS, c_t_take, gt[c * ZS + z] + gt_sib[z])
    grad_t[t] = back_rows(dir_t[...], norm_t[...], total)
    d_send(grad_t, d_t_ss, d_t_rs)
    total = lax.fori_loop(1, PS, c_i_take, gi[p])
    grad_i[t] = back_rows(dir_i[...], norm_i[...], total)
    d_send(grad_i, d_i_ss, d_i_rs)

    def weight_grad(grad, feat_ref, lane, width):
        g = lax.dot_general(
            grad[...].reshape(TS * R, E), feat_ref[...], (((0,), (0,)), ((), ())), preferred_element_type=f32
        )
        for k in range(2 * PS):
            g_ref[k % 2, k // 2, 0:OUT, lane:lane + width] = g[k * OUT:(k + 1) * OUT, :]

    d_take(grad_t, d_t_ss, d_t_rs)
    weight_grad(grad_t, ft_ref, DI, DT)
    d_take(grad_i, d_i_ss, d_i_rs)
    weight_grad(grad_i, fi_ref, 0, DI)
    g_copy = copy(g_ref.at[oc], g_sib, one_ss.at[2], one_rs.at[2], sibling)
    g_copy.start()
    g_copy.wait_recv()

    def e_copy(k, slot):
        return copy(e_out.at[k], e_in.at[slot], e_ss.at[k], e_rs.at[slot], column(k))

    def e_send(j, _):
        k = lax.rem(q + j, PS)
        e_out[k] = (g_ref[c, k] + g_sib[k]).astype(bf16)
        e_copy(k, q).start()
        return 0

    lax.fori_loop(1, PS, e_send, 0)

    def e_take(j, total):
        k = lax.rem(q + j, PS)
        e_copy(k, k).wait_recv()
        return total + e_in[k].astype(f32)

    out_ref[...] = lax.fori_loop(1, PS, e_take, g_ref[c, q] + g_sib[q])

    def sent_tensor(j, _):
        k = lax.rem(t + j, TS)
        a_copy(a_t_out, a_t_in, a_t_ss, a_t_rs, k, t).wait_send()
        a_copy(a_i_out, a_i_in, a_i_ss, a_i_rs, k, t).wait_send()
        d_copy(grad_t, d_t_ss, d_t_rs, k, t).wait_send()
        d_copy(grad_i, d_i_ss, d_i_rs, k, t).wait_send()
        return 0

    def sent_z(j, _):
        zz = lax.rem(z + j, ZS)
        b_t_copy(zz, z).wait_send()
        c_t_copy(zz, z).wait_send()
        return 0

    def sent_plane(j, _):
        k = lax.rem(p + j, PS)
        b_i_copy(k, p).wait_send()
        c_i_copy(k, p).wait_send()
        return 0

    def sent_column(j, _):
        e_copy(lax.rem(q + j, PS), q).wait_send()
        return 0

    def sent_relay(zz, _):
        relay(c, zz).wait_send()
        return 0

    lax.fori_loop(1, TS, sent_tensor, 0)
    lax.fori_loop(1, ZS, sent_z, 0)
    lax.fori_loop(1, PS, sent_plane, 0)
    lax.fori_loop(1, PS, sent_column, 0)
    lax.fori_loop(0, ZS, sent_relay, 0)
    pair_copy.wait_send()
    sib_copy.wait_send()
    g_copy.wait_send()


def on_device(image_features, text_features, image_weight, text_weight, image_pair, temp_index, bias_index):
    vmem = pl.BlockSpec(memory_space=pltpu.VMEM)
    smem = pl.BlockSpec(memory_space=pltpu.SMEM)
    dma = pltpu.SemaphoreType.DMA
    i16 = jnp.int16
    V = pltpu.VMEM
    acc = pl.pallas_call(
        kernel,
        out_shape=jax.ShapeDtypeStruct((OUT_ROWS, OUT_LANES), f32),
        in_specs=[smem, smem] + [vmem] * 5,
        out_specs=vmem,
        scratch_shapes=[
            V((TS, R, E), f32), V((TS, R, E), f32),
            V((TS, R, WIRE), i16), V((TS, R, WIRE), i16), V((TS, R, WIRE), i16), V((TS, R, WIRE), i16),
            V((R, E), f32), V((R, E), f32), V((R, 1), f32), V((R, 1), f32),
            V((PS, R, E), bf16), V((PS, R, E), bf16), V((8, 256), jnp.int32), V((8, 256), jnp.int32),
            V((PS * R, PS * R), bf16), V((PS, R, E), f32), V((PS, R, E), f32), V((ZS, R, E), f32), V((8, 128), f32),
            V((PS, R, WIRE), i16), V((PS, R, WIRE), i16), V((ZS, R, WIRE), i16), V((ZS, R, WIRE), i16),
            V((TS, R, E), bf16), V((TS, R, E), bf16),
            V((2, PS, OUT_ROWS, OUT_LANES), f32), V((PS, OUT_ROWS, OUT_LANES), f32), V((8, 128), f32),
            V((PS, OUT_ROWS, OUT_LANES), bf16), V((PS, OUT_ROWS, OUT_LANES), bf16),
        ]
        + [dma((TS,))] * 4 + [dma((PS,))] * 2 + [dma((ZS,))] * 4
        + [dma((PS,))] * 2 + [dma((ZS,))] * 2 + [dma((TS,))] * 4 + [dma((PS,))] * 2 + [dma((3,))] * 2,
        compiler_params=pltpu.CompilerParams(
            collective_id=0, has_side_effects=True, vmem_limit_bytes=50 * 2**20
        ),
        name="pair_loss_grads",
    )(
        temp_index.reshape(1), bias_index.reshape(1), image_pair.reshape(1, 256),
        image_features, text_features, image_weight, text_weight,
    )
    return acc[0:OUT, 0:DI].T, acc[0:OUT, DI:DI + DT].T


def solution(mesh):
    return jax.shard_map(
        on_device,
        mesh=mesh,
        in_specs=(P("dp", "tensor"), P("dp", "tensor"), P("tensor", None), P("tensor", None), P("dp"), P(), P()),
        out_specs=(P("tensor", "dp"), P("tensor", "dp")),
        check_vma=False,
    )
```

time: 746 us -> 112 us (0.15)
  waiting for transfers between devices: 673 us -> 0 us
  Pallas kernels: 0 us -> 105 us
  blocking collectives: 29.6 us -> 0 us
  matrix products: 14.2 us -> 0 us
  between operations: 16.2 us -> 2.04 us
  other arithmetic: 7.99 us -> 0 us
    unnamed x7 -> x0, waiting for transfers between devices: 228 us -> none
    reduce_scatter x2 -> x0, waiting for transfers between devices: 203 us -> none  [the longest x1 122 us: on_device(): lax.psum_scatter(lax.dot_general(weights, img_unit, contract, preferred_e...]
    psum x2 -> x0, waiting for transfers between devices: 173 us -> none  [the longest x1 88.1 us: on_device(): img = lax.psum(img_part, 'tensor')]
    pallas_call x0 -> x1, Pallas kernels: none -> 105 us  [on_device(): pl.pallas_call(kernel, out_shape=jax.ShapeDtypeStruct((OUT_ROWS, OUT_LANE...]
    all_gather x1 -> x0, waiting for transfers between devices: 69.2 us -> none  [on_device(): gathered = lax.all_gather(txt_unit, 'dp', axis=0, tiled=True)]
    all_gather x1 -> x0, blocking collectives: 29.6 us -> none  [on_device(): txt_grad = lax.all_gather(txt_grad_piece, 'tensor', axis=0, tiled=True)]
    dot_general x7 -> x0, matrix products: 14.2 us -> none  [the longest x1 3.05 us: on_device(): lax.dot_general(weights, img_unit, contract, preferred_element_type=jnp.f...]
  transfers between devices with their start and end apart: 6 -> 0, of which waited for: 6 -> 0; matrix products, arithmetic and copies ran while one was open for 2% -> 0% of each run, Pallas kernels for 0% -> 0%
where the time goes in v1:
time: 112 us
  Pallas kernels  105 us (94%)
  local copies, waits for them, and re-layouts  4.27 us (4%)
  between operations  2.04 us (2%)
    pallas_call x1, Pallas kernels, on_device(): pl.pallas_call(kernel, out_shape=jax.ShapeDtypeStruct((OUT_ROWS, OUT_LANE...  105 us
    unnamed x8, local copies, waits for them, and re-layouts  2.96 us

profile of v1, /device:TPU:1, one launch (start us, length us, event | category | flops | bytes accessed | tf_op | source)
XLA Modules:
  0.0 111.6 jit_solution(8305471722880026498)
XLA Ops:
  0.6 0.0 copy-start
  2.0 1.0 copy.9.fi_ref
  3.0 0.0 copy-start.2
  3.0 1.0 copy.10.ft_ref
  4.0 0.0 copy-done
  4.0 0.0 copy-done.2
  4.0 0.0 copy-start.1
  4.0 1.0 copy-done.1
  5.0 105.3 %pair_loss_grads.1 = f32[48,384]{1,0:T(8,128)S(1)} custom-call(s32[1]{0:T(128)} %bitcast.7.temp_ref, s32[1]{0:T(128)} %bitcast.8.bias_ref, s32[1,256]{1,0:T(1,128)S(1)} %bitcast.9, bf16[256,176]{1,0:T(8,128)(2,1)S(1)} %copy.9.fi_ref, bf16[256,144]{1,0:T(8,128)(2,1)S(1)} %copy.10.ft_ref, bf16[176,1152]{1,0:T(8,128)(2,1)S(1)} %copy-done, ...), custom_call_target="tpu_custom_call" | custom-call | tf_op jit(solution)/shard_map/pair_loss_grads/pallas_call | solution.py:364
  110.3 0.7 slice_bitcast_fusion
  111.0 0.6 slice_bitcast_fusion.1
Async XLA Ops:
  0.6 3.4 %copy-start = (bf16[176,1152]{1,0:T(8,128)(2,1)S(1)}, bf16[176,1152]{1,0:T(8,128)(2,1)}, u32[]{:S(2)}) copy-start(bf16[176,1152]{1,0:T(8,128)(2,1)} %wi_ref.1) | copy-start | bytes 1216516
  3.0 1.0 copy-start.2
  4.0 1.0 copy-start.1

commit v2 on v1

v2 whole, which is shorter than its diff:
```python
import jax
import jax.numpy as jnp
from jax import lax
from jax.experimental import pallas as pl
from jax.experimental.pallas import tpu as pltpu
from jax.sharding import PartitionSpec as P

MESH = pl.DeviceIdType.MESH
E = 1152
DI = 176
DT = 144
R = 32
TS = 8
ZS = 8
PS = 16
OUT = 36
XS = 4
H = 16
ROWS_I = 64
ROWS_T = 48
LEVELS = 32000.0
WIRE = E + 128
f32 = jnp.float32
bf16 = jnp.bfloat16


def encode(x):
    m = jnp.max(jnp.abs(x), axis=1, keepdims=True)
    hi = jnp.floor(m)
    lo = jnp.floor((m - hi) * LEVELS) + 1.0
    top = hi + lo * (1.0 / LEVELS)
    lane = lax.broadcasted_iota(jnp.int32, (x.shape[0], 128), 1)
    values = jnp.round(x * (LEVELS / top)).astype(jnp.int32).astype(jnp.int16)
    return values, jnp.where(lane < 64, hi, lo).astype(jnp.int32).astype(jnp.int16)


def put(wire, k, x):
    wire[k, :, 0:E], wire[k, :, E:WIRE] = encode(x)


def decode(wire, k):
    code = wire[k, :, E:WIRE].astype(jnp.int32).astype(f32)
    lane = lax.broadcasted_iota(jnp.int32, code.shape, 1)
    top = jnp.sum(jnp.where(lane < 64, code, code * (1.0 / LEVELS)), axis=1, keepdims=True) * (1.0 / 64)
    return wire[k, :, 0:E].astype(jnp.int32).astype(f32) * (top * (1.0 / LEVELS))


def unit_rows(values):
    norm = jnp.sqrt(jnp.sum(values * values, axis=1, keepdims=True) + 1e-06)
    return norm, values / norm


def back_rows(direct, norm, grad):
    inner = jnp.sum(direct * grad, axis=1, keepdims=True)
    return ((grad - direct * inner) / norm).astype(bf16)


def kernel(
    temp_ref, bias_ref, pair_hbm, fi_hbm, ft_hbm, wi_hbm, wt_hbm, out_ref,
    fi_ref, ft_ref, wi_ref, wt_ref,
    part_i, part_t, a_i_out, a_i_in, a_t_out, a_t_in,
    dir_i, dir_t, norm_i, norm_t, unit_0, unit_1, all_t, pair_out, pair_in, target_ref,
    w_ref, gi_0, gi_1, gt, gt_sib, ca_out_0, ca_in_0, ca_out_1, ca_in_1,
    half_0, half_1, cb_out_0, cb_in_0, cb_out_1, cb_in_1, c_t_out, c_t_in,
    grad_i, grad_t, g_i, g_t, sib_i, sib_t, e_i_out, e_i_in, e_t_out, e_t_in,
    load_s, a_i_ss, a_i_rs, a_t_ss, a_t_rs, ba_ss, ba_rs, bb_ss, bb_rs, b_t_ss, b_t_rs, relay_ss, relay_rs,
    ca_ss, ca_rs, cb_ss, cb_rs, c_t_ss, c_t_rs, d_i_ss, d_i_rs, d_t_ss, d_t_rs,
    e_i_ss, e_i_rs, e_t_ss, e_t_rs, one_ss, one_rs,
):
    loads = [
        pltpu.make_async_copy(src, dst, load_s.at[k])
        for k, (src, dst) in enumerate((
            (ft_hbm, ft_ref), (wt_hbm, wt_ref), (fi_hbm, fi_ref), (wi_hbm, wi_ref), (pair_hbm, pair_out.at[0:1])
        ))
    ]
    for load in loads:
        load.start()

    dp = lax.axis_index("dp")
    t = lax.axis_index("tensor")
    ylo = lax.div(dp, 16)
    z = lax.rem(lax.div(dp, 2), 8)
    c = lax.rem(dp, 2)
    oc = 1 - c
    yhi = lax.div(t, XS)
    x = lax.rem(t, XS)
    y = yhi * 2 + ylo
    q = ylo * ZS + z

    def device(ylo_, z_, c_, t_):
        return ((ylo_ * ZS + z_) * 2 + c_, t_)

    sibling = device(ylo, z, oc, t)
    across = device(1 - ylo, z, c, t)
    beyond = device(1 - ylo, z, c, (1 - yhi) * XS + x)

    def at_x(xx):
        return (dp, yhi * XS + xx)

    def at_y(yy):
        return device(lax.rem(yy, 2), z, c, lax.div(yy, 2) * XS + x)

    def column(k):
        return device(lax.div(k, ZS), lax.rem(k, ZS), c, t)

    def tensor_peer(j):
        j = lax.rem(j * 5, TS)
        return lax.rem(yhi + lax.div(j, XS), 2) * XS + lax.rem(x + lax.rem(j, XS), XS)

    def z_peer(j):
        return lax.rem(z + j * 3, ZS)

    def column_peer(j):
        j = lax.rem(j * 7, PS)
        return lax.rem(ylo + lax.div(j, ZS), 2) * ZS + lax.rem(z + lax.rem(j, ZS), ZS)

    def copy(src, dst, ssem, rsem, dev):
        return pltpu.make_async_remote_copy(
            src_ref=src, dst_ref=dst, send_sem=ssem, recv_sem=rsem, device_id=dev, device_id_type=MESH
        )

    barrier = pltpu.get_barrier_semaphore()

    def greet(dev):
        pl.semaphore_signal(barrier, inc=1, device_id=dev, device_id_type=MESH)

    def greet_tensor(j, _):
        greet((dp, tensor_peer(j)))
        return 0

    def greet_column(j, _):
        greet(column(column_peer(j)))
        return 0

    lax.fori_loop(1, TS, greet_tensor, 0)
    lax.fori_loop(1, PS, greet_column, 0)
    greet(beyond)
    greet(sibling)

    def product(feat, weight):
        return lax.dot_general(
            feat[...], weight[...], (((0,), (0,)), ((), ())), preferred_element_type=f32
        ).reshape(TS, R, E)

    g_i[...] = jnp.zeros_like(g_i)
    g_t[...] = jnp.zeros_like(g_t)
    loads[0].wait()
    loads[1].wait()
    part_t[...] = product(ft_ref, wt_ref)
    loads[4].wait()
    pair_out[...] = jnp.broadcast_to(pair_out[0:1, :], (8, 256))
    pl.semaphore_wait(barrier, (TS - 1) + (PS - 1) + 2)

    def a_copy(wire_out, wire_in, ss, rs, k, slot):
        return copy(wire_out.at[k], wire_in.at[slot], ss.at[k], rs.at[slot], (dp, k))

    def a_send(part, wire_out, wire_in, ss, rs):
        def step(j, _):
            k = tensor_peer(j)
            put(wire_out, k, part[k])
            a_copy(wire_out, wire_in, ss, rs, k, t).start()
            return 0
        lax.fori_loop(1, TS, step, 0)

    def a_take(part, wire_out, wire_in, ss, rs):
        def step(j, total):
            k = tensor_peer(TS - j)
            a_copy(wire_out, wire_in, ss, rs, k, k).wait_recv()
            return total + decode(wire_in, k)
        return lax.fori_loop(1, TS, step, part[t])

    a_send(part_t, a_t_out, a_t_in, a_t_ss, a_t_rs)
    pair_copy = copy(pair_out, pair_in, one_ss.at[0], one_rs.at[0], across)
    pair_copy.start()
    loads[2].wait()
    loads[3].wait()
    part_i[...] = product(fi_ref, wi_ref)
    a_send(part_i, a_i_out, a_i_in, a_i_ss, a_i_rs)

    def local_target(pair):
        r = pair & 31
        tt = (pair >> 5) & 7
        cc = (pair >> 8) & 1
        zz = (pair >> 9) & 7
        yy = (pair >> 12) & 1
        here = jnp.logical_and(tt == t, yy == ylo)
        return jnp.where(here, (cc * ZS + zz) * R + r, -1)

    pair_copy.wait_recv()
    own = local_target(pair_out[0:1, :])
    other = local_target(pair_in[0:1, :])
    by_ylo = (jnp.where(ylo == 0, own, other), jnp.where(ylo == 0, other, own))
    for yy in range(XS):
        for xx in range(XS):
            lane = ((yy // 2) * XS + xx) * R
            s0, s1 = (yy * XS + xx) * H, (xx * XS + yy) * H + PS * H
            target_ref[0:1, s0:s0 + H] = by_ylo[yy % 2][:, lane:lane + H]
            target_ref[0:1, s1:s1 + H] = by_ylo[yy % 2][:, lane + H:lane + R]

    def b_t_copy(zz, slot):
        s = c * ZS + slot
        return copy(all_t.at[s], all_t.at[s], b_t_ss.at[zz], b_t_rs.at[slot], device(ylo, zz, c, t))

    def relay(cc, zz):
        s = cc * ZS + zz
        return copy(all_t.at[s], all_t.at[s], relay_ss.at[zz], relay_rs.at[zz], sibling)

    norm, direct = unit_rows(a_take(part_t, a_t_out, a_t_in, a_t_ss, a_t_rs))
    norm_t[...] = norm
    dir_t[...] = direct
    all_t[c * ZS + z] = direct.astype(bf16)

    def b_t_send(j, _):
        b_t_copy(z_peer(j), z).start()
        return 0

    lax.fori_loop(1, ZS, b_t_send, 0)
    relay(c, z).start()

    halves = ((unit_0, at_x, x, at_y, y), (unit_1, at_y, y, at_x, x))

    def ba_copy(h, k, slot):
        unit, first, me, second, line = halves[h]
        s = line * XS + slot
        return copy(unit.at[s], unit.at[s], ba_ss.at[h * XS + k], ba_rs.at[h * XS + slot], first(k))

    def bb_copy(h, k, slot):
        unit, first, me, second, line = halves[h]
        s = pl.ds(slot * XS, XS)
        return copy(unit.at[s], unit.at[s], bb_ss.at[h * XS + k], bb_rs.at[h * XS + slot], second(k))

    norm, direct = unit_rows(a_take(part_i, a_i_out, a_i_in, a_i_ss, a_i_rs))
    norm_i[...] = norm
    dir_i[...] = direct
    unit = direct.astype(bf16)
    unit_0[y * XS + x] = unit[0:H]
    unit_1[x * XS + y] = unit[H:R]
    steps = [(d, h) for d in (2, 1, 3) for h in (0, 1)]
    for d, h in steps:
        me = halves[h][2]
        ba_copy(h, lax.rem(me + d, XS), me).start()
    for h in (0, 1):
        me, line = halves[h][2], halves[h][4]
        for d in (1, 3, 2):
            k = lax.rem(me + d, XS)
            ba_copy(h, k, k).wait_recv()
        for d in (2, 1, 3):
            bb_copy(h, lax.rem(line + d, XS), line).start()

    def b_t_take(j, _):
        zz = z_peer(ZS - j)
        b_t_copy(zz, zz).wait_recv()
        relay(c, zz).start()
        return 0

    lax.fori_loop(1, ZS, b_t_take, 0)

    def relay_take(zz, _):
        relay(oc, zz).wait_recv()
        return 0

    lax.fori_loop(0, ZS, relay_take, 0)
    for d, h in steps:
        k = lax.rem(halves[h][4] + d, XS)
        bb_copy(h, k, k).wait_recv()

    scale = 4.0 + temp_ref[0].astype(f32)
    shift = -0.5 * bias_ref[0].astype(f32)
    half = PS * H

    def tile(j, _):
        b = lax.rem(2 * oc + j, 4)
        rows = all_t[pl.ds(b * 4, 4)].reshape(4 * R, E)
        total = None
        for h, unit in ((0, unit_0), (1, unit_1)):
            img = unit[...].reshape(half, E)
            logits = scale * lax.dot_general(
                rows, img, (((1,), (1,)), ((), ())), preferred_element_type=f32
            ) + shift
            index = lax.broadcasted_iota(jnp.int32, (4 * R, half), 0) + b * (4 * R)
            sign = jnp.where(index == target_ref[0:1, h * half:(h + 1) * half], f32(1.0), f32(-1.0))
            w = (-scale * sign * jax.nn.sigmoid(-sign * logits)).astype(bf16)
            w_ref[pl.ds(pl.multiple_of(b * (4 * R), 4 * R), 4 * R), h * half:(h + 1) * half] = w
            part = jnp.dot(w, img, preferred_element_type=f32)
            total = part if total is None else total + part
        gt[pl.ds(b * 4, 4)] = total.reshape(4, R, E)
        return 0

    lax.fori_loop(0, 2, tile, 0)
    gt_copy = copy(gt.at[pl.ds(oc * ZS, ZS)], gt_sib, one_ss.at[1], one_rs.at[1], sibling)
    gt_copy.start()
    lax.fori_loop(2, 4, tile, 0)
    gt_copy.wait_recv()

    def c_t_copy(zz, slot):
        return copy(c_t_out.at[zz], c_t_in.at[slot], c_t_ss.at[zz], c_t_rs.at[slot], device(ylo, zz, c, t))

    def c_t_send(j, _):
        zz = z_peer(j)
        put(c_t_out, zz, gt[c * ZS + zz] + gt_sib[zz])
        c_t_copy(zz, z).start()
        return 0

    lax.fori_loop(1, ZS, c_t_send, 0)

    back = ((gi_0, ca_out_0, ca_in_0, half_0, cb_out_0, cb_in_0), (gi_1, ca_out_1, ca_in_1, half_1, cb_out_1, cb_in_1))

    def ca_copy(h, k, slot):
        out, into = back[h][1], back[h][2]
        return copy(out.at[k], into.at[slot], ca_ss.at[h * XS + k], ca_rs.at[h * XS + slot], halves[h][3](k))

    def cb_copy(h, k, slot):
        out, into = back[h][4], back[h][5]
        return copy(out.at[k], into.at[slot], cb_ss.at[h * XS + k], cb_rs.at[h * XS + slot], halves[h][1](k))

    for h in (0, 1):
        gi, out = back[h][0], back[h][1]
        for b in range(2):
            lane = h * half + b * 128
            gi[8 * b:8 * b + 8] = lax.dot_general(
                w_ref[:, lane:lane + 128], all_t[...].reshape(PS * R, E), (((0,), (0,)), ((), ())),
                preferred_element_type=f32,
            ).reshape(8, H, E)
        line = halves[h][4]
        for d in (2, 1, 3):
            k = lax.rem(line + d, XS)
            put(out, k, gi[pl.ds(k * XS, XS)].reshape(XS * H, E))
            ca_copy(h, k, line).start()

    for h in (0, 1):
        gi, into, part, out = back[h][0], back[h][2], back[h][3], back[h][4]
        me, line = halves[h][2], halves[h][4]
        total = gi[pl.ds(line * XS, XS)].reshape(XS * H, E)
        for d in (1, 3, 2):
            k = lax.rem(line + d, XS)
            ca_copy(h, k, k).wait_recv()
            total = total + decode(into, k)
        part[...] = total.reshape(XS, H, E)
        for d in (2, 1, 3):
            k = lax.rem(me + d, XS)
            put(out, k, part[k])
            cb_copy(h, k, me).start()

    def c_i_take(h):
        into, part, me = back[h][5], back[h][3], halves[h][2]
        total = part[me]
        for d in (1, 3, 2):
            k = lax.rem(me + d, XS)
            cb_copy(h, k, k).wait_recv()
            total = total + decode(into, k)
        return total

    def c_t_take(j, total):
        zz = z_peer(ZS - j)
        c_t_copy(zz, zz).wait_recv()
        return total + decode(c_t_in, zz)

    def d_copy(grad, ss, rs, k, slot):
        return copy(grad.at[slot], grad.at[slot], ss.at[k], rs.at[slot], (dp, k))

    def d_send(grad, ss, rs):
        def step(j, _):
            d_copy(grad, ss, rs, tensor_peer(j), t).start()
            return 0
        lax.fori_loop(1, TS, step, 0)

    def d_take(grad, ss, rs):
        def step(j, _):
            k = tensor_peer(TS - j)
            d_copy(grad, ss, rs, k, k).wait_recv()
            return 0
        lax.fori_loop(1, TS, step, 0)

    total = jnp.concatenate([c_i_take(0), c_i_take(1)], axis=0)
    grad_i[t] = back_rows(dir_i[...], norm_i[...], total)
    d_send(grad_i, d_i_ss, d_i_rs)
    total = lax.fori_loop(1, ZS, c_t_take, gt[c * ZS + z] + gt_sib[z])
    grad_t[t] = back_rows(dir_t[...], norm_t[...], total)
    d_send(grad_t, d_t_ss, d_t_rs)

    def weight_grad(grad, feat, packed, fold):
        g = lax.dot_general(
            grad[...].reshape(TS * R, E), feat[...], (((0,), (1,)), ((), ())), preferred_element_type=f32
        )
        rest, rows = g.shape[1] - 128, OUT // fold
        for k in range(2 * PS):
            packed[k % 2, k // 2, 0:OUT, :] = g[k * OUT:(k + 1) * OUT, 0:128]
            for n in range(fold):
                packed[k % 2, k // 2, OUT:OUT + rows, n * rest:(n + 1) * rest] = (
                    g[k * OUT + n * rows:k * OUT + (n + 1) * rows, 128:]
                )

    def e_copy(out, into, ss, rs, k, slot):
        return copy(out.at[k], into.at[slot], ss.at[k], rs.at[slot], column(k))

    def e_send(packed, sib, out, into, ss, rs):
        def step(j, _):
            k = column_peer(j)
            out[k] = (packed[c, k] + sib[k]).astype(bf16)
            e_copy(out, into, ss, rs, k, q).start()
            return 0
        lax.fori_loop(1, PS, step, 0)

    def e_take(packed, sib, out, into, ss, rs):
        def step(j, total):
            k = column_peer(PS - j)
            e_copy(out, into, ss, rs, k, k).wait_recv()
            return total + into[k].astype(f32)
        return lax.fori_loop(1, PS, step, packed[c, q] + sib[q])

    e_i = (g_i, sib_i, e_i_out, e_i_in, e_i_ss, e_i_rs)
    e_t = (g_t, sib_t, e_t_out, e_t_in, e_t_ss, e_t_rs)
    d_take(grad_i, d_i_ss, d_i_rs)
    weight_grad(grad_i, fi_ref, g_i, 2)
    g_i_copy = copy(g_i.at[oc], sib_i, one_ss.at[2], one_rs.at[2], sibling)
    g_i_copy.start()
    g_i_copy.wait_recv()
    e_send(*e_i)
    d_take(grad_t, d_t_ss, d_t_rs)
    weight_grad(grad_t, ft_ref, g_t, 3)
    g_t_copy = copy(g_t.at[oc], sib_t, one_ss.at[3], one_rs.at[3], sibling)
    g_t_copy.start()
    g_t_copy.wait_recv()
    e_send(*e_t)

    def unpack(total, lane, width, fold):
        rest, rows = width - 128, OUT // fold
        out_ref[0:OUT, lane:lane + 128] = total[0:OUT, :]
        for n in range(fold):
            out_ref[n * rows:(n + 1) * rows, lane + 128:lane + width] = (
                total[OUT:OUT + rows, n * rest:(n + 1) * rest]
            )

    unpack(e_take(*e_i), 0, DI, 2)
    unpack(e_take(*e_t), 256, DT, 3)

    def sent_tensor(j, _):
        k = tensor_peer(j)
        a_copy(a_t_out, a_t_in, a_t_ss, a_t_rs, k, t).wait_send()
        a_copy(a_i_out, a_i_in, a_i_ss, a_i_rs, k, t).wait_send()
        d_copy(grad_t, d_t_ss, d_t_rs, k, t).wait_send()
        d_copy(grad_i, d_i_ss, d_i_rs, k, t).wait_send()
        return 0

    def sent_z(j, _):
        zz = z_peer(j)
        b_t_copy(zz, z).wait_send()
        c_t_copy(zz, z).wait_send()
        return 0

    def sent_column(j, _):
        k = column_peer(j)
        e_copy(e_i_out, e_i_in, e_i_ss, e_i_rs, k, q).wait_send()
        e_copy(e_t_out, e_t_in, e_t_ss, e_t_rs, k, q).wait_send()
        return 0

    def sent_relay(zz, _):
        relay(c, zz).wait_send()
        return 0

    lax.fori_loop(1, TS, sent_tensor, 0)
    lax.fori_loop(1, ZS, sent_z, 0)
    lax.fori_loop(1, PS, sent_column, 0)
    lax.fori_loop(0, ZS, sent_relay, 0)
    for d, h in steps:
        me, line = halves[h][2], halves[h][4]
        ba_copy(h, lax.rem(me + d, XS), me).wait_send()
        bb_copy(h, lax.rem(line + d, XS), line).wait_send()
        ca_copy(h, lax.rem(line + d, XS), line).wait_send()
        cb_copy(h, lax.rem(me + d, XS), me).wait_send()
    for sent in (pair_copy, gt_copy, g_i_copy, g_t_copy):
        sent.wait_send()


def on_device(image_features, text_features, image_weight, text_weight, image_pair, temp_index, bias_index):
    vmem = pl.BlockSpec(memory_space=pltpu.VMEM)
    smem = pl.BlockSpec(memory_space=pltpu.SMEM)
    hbm = pl.BlockSpec(memory_space=pl.ANY)
    dma = pltpu.SemaphoreType.DMA
    i16 = jnp.int16
    V = pltpu.VMEM
    acc = pl.pallas_call(
        kernel,
        out_shape=jax.ShapeDtypeStruct((40, 512), f32),
        in_specs=[smem, smem] + [hbm] * 5,
        out_specs=vmem,
        scratch_shapes=[
            V((DI, 256), bf16), V((DT, 256), bf16), V((DI, E), bf16), V((DT, E), bf16),
            V((TS, R, E), f32), V((TS, R, E), f32),
            V((TS, R, WIRE), i16), V((TS, R, WIRE), i16), V((TS, R, WIRE), i16), V((TS, R, WIRE), i16),
            V((R, E), f32), V((R, E), f32), V((R, 1), f32), V((R, 1), f32),
            V((PS, H, E), bf16), V((PS, H, E), bf16), V((PS, R, E), bf16),
            V((8, 256), jnp.int32), V((8, 256), jnp.int32), V((8, PS * R), jnp.int32),
            V((PS * R, PS * R), bf16), V((PS, H, E), f32), V((PS, H, E), f32), V((PS, R, E), f32), V((ZS, R, E), f32),
        ]
        + [V((XS, XS * H, WIRE), i16)] * 4
        + [V((XS, H, E), f32)] * 2 + [V((XS, H, WIRE), i16)] * 4 + [V((ZS, R, WIRE), i16)] * 2
        + [
            V((TS, R, E), bf16), V((TS, R, E), bf16),
            V((2, PS, ROWS_I, 128), f32), V((2, PS, ROWS_T, 128), f32),
            V((PS, ROWS_I, 128), f32), V((PS, ROWS_T, 128), f32),
            V((PS, ROWS_I, 128), bf16), V((PS, ROWS_I, 128), bf16),
            V((PS, ROWS_T, 128), bf16), V((PS, ROWS_T, 128), bf16),
        ]
        + [dma((5,))] + [dma((TS,))] * 4 + [dma((2 * XS,))] * 4 + [dma((ZS,))] * 4
        + [dma((2 * XS,))] * 4 + [dma((ZS,))] * 2 + [dma((TS,))] * 4 + [dma((PS,))] * 4 + [dma((4,))] * 2,
        compiler_params=pltpu.CompilerParams(
            collective_id=0, has_side_effects=True, vmem_limit_bytes=56 * 2**20
        ),
        name="pair_loss_grads",
    )(
        temp_index.reshape(1), bias_index.reshape(1), image_pair.reshape(1, 256),
        image_features.T, text_features.T, image_weight, text_weight,
    )
    return acc[0:OUT, 0:DI].T, acc[0:OUT, 256:256 + DT].T


def solution(mesh):
    return jax.shard_map(
        on_device,
        mesh=mesh,
        in_specs=(P("dp", "tensor"), P("dp", "tensor"), P("tensor", None), P("tensor", None), P("dp"), P(), P()),
        out_specs=(P("tensor", "dp"), P("tensor", "dp")),
        check_vma=False,
    )
```

time: 112 us -> 94 us (0.84)
  Pallas kernels: 105 us -> 89.9 us
  local copies, waits for them, and re-layouts: 4.27 us -> 2.09 us
    pallas_call x1, Pallas kernels: 105 us -> 89.9 us  [on_device(): pl.pallas_call(kernel, out_shape=jax.ShapeDtypeStruct((40, 512), f32), in...]
    unnamed x8 -> x2, local copies, waits for them, and re-layouts: 2.96 us -> 0.01 us
where the time goes in v2:
time: 94 us; the launch traced here: 93.9 us
  Pallas kernels  89.9 us (96%)
  local copies, waits for them, and re-layouts  2.09 us (2%)
  between operations  1.94 us (2%)
    pallas_call x1, Pallas kernels, on_device(): pl.pallas_call(kernel, out_shape=jax.ShapeDtypeStruct((40, 512), f32), in...  89.9 us
    transpose x2, local copies, waits for them, and re-layouts, on_device(): return (acc[0:OUT, 0:DI].T, acc[0:OUT, 256:256 + DT].T)  2.08 us

profile of v2, /device:TPU:1, one launch (start us, length us, event | category | flops | bytes accessed | tf_op | source)
XLA Modules:
  0.0 93.9 jit_solution(11290007139642924065)
XLA Ops:
  1.9 89.9 %pair_loss_grads.1 = f32[40,512]{1,0:T(8,128)} custom-call(s32[1]{0:T(128)} %bitcast.9.temp_ref, s32[1]{0:T(128)} %bitcast.10.bias_ref, s32[1,256]{1,0:T(1,128)} %bitcast.13, bf16[176,256]{1,0:T(8,128)(2,1)} %bitcast.11, bf16[144,256]{1,0:T(8,128)(2,1)} %bitcast.12, bf16[176,1152]{1,0:T(8,128)(2,1)} %wi_hbm.1, bf16[144,1152]{1,0:T(8,128)(2,1)} %wt_hbm.1), custom_call_target="tpu_custom_call" | custom-call | tf_op jit(solution)/shard_map/pair_loss_grads/pallas_call | solution.py:482
  91.8 0.0 copy-start
  91.8 1.5 %slice_bitcast_fusion = f32[144,36]{0,1:T(8,128)} fusion(f32[40,512]{1,0:T(8,128)} %pair_loss_grads.1), kind=kLoop, calls=%fused_computation | loop fusion | bytes 41472 | tf_op jit(solution)/shard_map/transpose | solution.py:515
  93.3 0.0 copy-done
  93.3 0.6 slice_bitcast_fusion.1
Async XLA Ops:
  91.8 1.5 %copy-start = (f32[40,512]{1,0:T(8,128)S(1)}, f32[40,512]{1,0:T(8,128)}, u32[]{:S(2)}) copy-start(f32[40,512]{1,0:T(8,128)} %pair_loss_grads.1) | copy-start | bytes 245764

commit v3 on v2

--- a/solution.py
+++ b/solution.py
@@ -19,30 +19,36 @@
 ROWS_I = 64
 ROWS_T = 48
 LEVELS = 32000.0
-WIRE = E + 128
+G = E // 128
 f32 = jnp.float32
 bf16 = jnp.bfloat16
 
 
-def encode(x):
+def put(wire, k, x):
+    n = x.shape[0]
     m = jnp.max(jnp.abs(x), axis=1, keepdims=True)
     hi = jnp.floor(m)
     lo = jnp.floor((m - hi) * LEVELS) + 1.0
-    top = hi + lo * (1.0 / LEVELS)
-    lane = lax.broadcasted_iota(jnp.int32, (x.shape[0], 128), 1)
-    values = jnp.round(x * (LEVELS / top)).astype(jnp.int32).astype(jnp.int16)
-    return values, jnp.where(lane < 64, hi, lo).astype(jnp.int32).astype(jnp.int16)
-
-
-def put(wire, k, x):
-    wire[k, :, 0:E], wire[k, :, E:WIRE] = encode(x)
-
-
-def decode(wire, k):
-    code = wire[k, :, E:WIRE].astype(jnp.int32).astype(f32)
-    lane = lax.broadcasted_iota(jnp.int32, code.shape, 1)
-    top = jnp.sum(jnp.where(lane < 64, code, code * (1.0 / LEVELS)), axis=1, keepdims=True) * (1.0 / 64)
-    return wire[k, :, 0:E].astype(jnp.int32).astype(f32) * (top * (1.0 / LEVELS))
+    q = jnp.round(x * (LEVELS / (hi + lo * (1.0 / LEVELS)))).astype(jnp.int32).astype(jnp.int16)
+    for g in range(G):
+        wire[k, g * n:(g + 1) * n, :] = q[:, g * 128:(g + 1) * 128]
+    diagonal = lax.broadcasted_iota(jnp.int32, (n, 128), 0) == lax.broadcasted_iota(jnp.int32, (n, 128), 1)
+    hi = jnp.sum(jnp.where(diagonal, hi, 0.0), axis=0, keepdims=True)
+    lo = jnp.sum(jnp.where(diagonal, lo, 0.0), axis=0, keepdims=True)
+    row = lax.broadcasted_iota(jnp.int32, (16, 128), 0)
+    wire[k, G * n:G * n + 16, :] = (
+        jnp.where(row == 0, hi, jnp.where(row == 1, lo, 0.0)).astype(jnp.int32).astype(jnp.int16)
+    )
+
+
+def take(wire, k, n):
+    code = wire[k, G * n:G * n + 16, :].astype(jnp.int32).astype(f32)
+    top = code[0:1, :] + code[1:2, :] * (1.0 / LEVELS)
+    diagonal = lax.broadcasted_iota(jnp.int32, (n, 128), 0) == lax.broadcasted_iota(jnp.int32, (n, 128), 1)
+    step = jnp.sum(jnp.where(diagonal, top, 0.0), axis=1, keepdims=True) * (1.0 / LEVELS)
+    return jnp.concatenate(
+        [wire[k, g * n:(g + 1) * n, :].astype(jnp.int32).astype(f32) * step for g in range(G)], axis=1
+    )
 
 
 def unit_rows(values):
@@ -56,7 +62,8 @@
 
 
 def kernel(
-    temp_ref, bias_ref, pair_hbm, fi_hbm, ft_hbm, wi_hbm, wt_hbm, out_ref,
+    temp_hbm, bias_hbm, pair_hbm, fi_hbm, ft_hbm, wi_hbm, wt_hbm, out_i, out_t,
+    temp_ref, bias_ref,
     fi_ref, ft_ref, wi_ref, wt_ref,
     part_i, part_t, a_i_out, a_i_in, a_t_out, a_t_in,
     dir_i, dir_t, norm_i, norm_t, unit_0, unit_1, all_t, pair_out, pair_in, target_ref,
@@ -64,13 +71,14 @@
     half_0, half_1, cb_out_0, cb_in_0, cb_out_1, cb_in_1, c_t_out, c_t_in,
     grad_i, grad_t, g_i, g_t, sib_i, sib_t, e_i_out, e_i_in, e_t_out, e_t_in,
     load_s, a_i_ss, a_i_rs, a_t_ss, a_t_rs, ba_ss, ba_rs, bb_ss, bb_rs, b_t_ss, b_t_rs, relay_ss, relay_rs,
-    ca_ss, ca_rs, cb_ss, cb_rs, c_t_ss, c_t_rs, d_i_ss, d_i_rs, d_t_ss, d_t_rs,
+    ca_ss, ca_rs, cb_ss, cb_rs, gt_ss, gt_rs, c_t_ss, c_t_rs, d_i_ss, d_i_rs, d_t_ss, d_t_rs,
     e_i_ss, e_i_rs, e_t_ss, e_t_rs, one_ss, one_rs,
 ):
     loads = [
         pltpu.make_async_copy(src, dst, load_s.at[k])
         for k, (src, dst) in enumerate((
-            (ft_hbm, ft_ref), (wt_hbm, wt_ref), (fi_hbm, fi_ref), (wi_hbm, wi_ref), (pair_hbm, pair_out.at[0:1])
+            (ft_hbm, ft_ref), (wt_hbm, wt_ref), (fi_hbm, fi_ref), (wi_hbm, wi_ref), (pair_hbm, pair_out.at[0:1]),
+            (temp_hbm, temp_ref), (bias_hbm, bias_ref),
         ))
     ]
     for load in loads:
@@ -166,7 +174,7 @@
         def step(j, total):
             k = tensor_peer(TS - j)
             a_copy(wire_out, wire_in, ss, rs, k, k).wait_recv()
-            return total + decode(wire_in, k)
+            return total + take(wire_in, k, R)
         return lax.fori_loop(1, TS, step, part[t])
 
     a_send(part_t, a_t_out, a_t_in, a_t_ss, a_t_rs)
@@ -224,10 +232,10 @@
         s = line * XS + slot
         return copy(unit.at[s], unit.at[s], ba_ss.at[h * XS + k], ba_rs.at[h * XS + slot], first(k))
 
-    def bb_copy(h, k, slot):
+    def bb_copy(h, i, k, slot):
         unit, first, me, second, line = halves[h]
-        s = pl.ds(slot * XS, XS)
-        return copy(unit.at[s], unit.at[s], bb_ss.at[h * XS + k], bb_rs.at[h * XS + slot], second(k))
+        s = slot * XS + i
+        return copy(unit.at[s], unit.at[s], bb_ss.at[h * PS + k * XS + i], bb_rs.at[h * PS + s], second(k))
 
     norm, direct = unit_rows(a_take(part_i, a_i_out, a_i_in, a_i_ss, a_i_rs))
     norm_i[...] = norm
@@ -239,13 +247,19 @@
     for d, h in steps:
         me = halves[h][2]
         ba_copy(h, lax.rem(me + d, XS), me).start()
+
+    def bb_send(h, i):
+        line = halves[h][4]
+        for d in (2, 1, 3):
+            bb_copy(h, i, lax.rem(line + d, XS), line).start()
+
     for h in (0, 1):
-        me, line = halves[h][2], halves[h][4]
-        for d in (1, 3, 2):
-            k = lax.rem(me + d, XS)
+        bb_send(h, halves[h][2])
+    for d in (1, 3, 2):
+        for h in (0, 1):
+            k = lax.rem(halves[h][2] + d, XS)
             ba_copy(h, k, k).wait_recv()
-        for d in (2, 1, 3):
-            bb_copy(h, lax.rem(line + d, XS), line).start()
+            bb_send(h, k)
 
     def b_t_take(j, _):
         zz = z_peer(ZS - j)
@@ -262,98 +276,126 @@
     lax.fori_loop(0, ZS, relay_take, 0)
     for d, h in steps:
         k = lax.rem(halves[h][4] + d, XS)
-        bb_copy(h, k, k).wait_recv()
-
+        for i in range(XS):
+            bb_copy(h, i, k, k).wait_recv()
+
+    loads[5].wait()
+    loads[6].wait()
     scale = 4.0 + temp_ref[0].astype(f32)
     shift = -0.5 * bias_ref[0].astype(f32)
     half = PS * H
 
-    def tile(j, _):
-        b = lax.rem(2 * oc + j, 4)
+    def tile_weights(b, _):
         rows = all_t[pl.ds(b * 4, 4)].reshape(4 * R, E)
-        total = None
         for h, unit in ((0, unit_0), (1, unit_1)):
-            img = unit[...].reshape(half, E)
             logits = scale * lax.dot_general(
-                rows, img, (((1,), (1,)), ((), ())), preferred_element_type=f32
+                rows, unit[...].reshape(half, E), (((1,), (1,)), ((), ())), preferred_element_type=f32
             ) + shift
             index = lax.broadcasted_iota(jnp.int32, (4 * R, half), 0) + b * (4 * R)
             sign = jnp.where(index == target_ref[0:1, h * half:(h + 1) * half], f32(1.0), f32(-1.0))
             w = (-scale * sign * jax.nn.sigmoid(-sign * logits)).astype(bf16)
             w_ref[pl.ds(pl.multiple_of(b * (4 * R), 4 * R), 4 * R), h * half:(h + 1) * half] = w
-            part = jnp.dot(w, img, preferred_element_type=f32)
-            total = part if total is None else total + part
-        gt[pl.ds(b * 4, 4)] = total.reshape(4, R, E)
-        return 0
-
-    lax.fori_loop(0, 2, tile, 0)
-    gt_copy = copy(gt.at[pl.ds(oc * ZS, ZS)], gt_sib, one_ss.at[1], one_rs.at[1], sibling)
-    gt_copy.start()
-    lax.fori_loop(2, 4, tile, 0)
-    gt_copy.wait_recv()
-
-    def c_t_copy(zz, slot):
-        return copy(c_t_out.at[zz], c_t_in.at[slot], c_t_ss.at[zz], c_t_rs.at[slot], device(ylo, zz, c, t))
-
-    def c_t_send(j, _):
-        zz = z_peer(j)
-        put(c_t_out, zz, gt[c * ZS + zz] + gt_sib[zz])
-        c_t_copy(zz, z).start()
-        return 0
-
-    lax.fori_loop(1, ZS, c_t_send, 0)
+        return 0
+
+    lax.fori_loop(0, 4, tile_weights, 0)
 
     back = ((gi_0, ca_out_0, ca_in_0, half_0, cb_out_0, cb_in_0), (gi_1, ca_out_1, ca_in_1, half_1, cb_out_1, cb_in_1))
 
-    def ca_copy(h, k, slot):
+    def ca_copy(h, i, k, slot):
         out, into = back[h][1], back[h][2]
-        return copy(out.at[k], into.at[slot], ca_ss.at[h * XS + k], ca_rs.at[h * XS + slot], halves[h][3](k))
+        return copy(
+            out.at[k * XS + i], into.at[slot * XS + i],
+            ca_ss.at[h * PS + k * XS + i], ca_rs.at[h * PS + slot * XS + i], halves[h][3](k),
+        )
 
     def cb_copy(h, k, slot):
         out, into = back[h][4], back[h][5]
         return copy(out.at[k], into.at[slot], cb_ss.at[h * XS + k], cb_rs.at[h * XS + slot], halves[h][1](k))
 
     for h in (0, 1):
-        gi, out = back[h][0], back[h][1]
+        gi = back[h][0]
         for b in range(2):
             lane = h * half + b * 128
             gi[8 * b:8 * b + 8] = lax.dot_general(
                 w_ref[:, lane:lane + 128], all_t[...].reshape(PS * R, E), (((0,), (0,)), ((), ())),
                 preferred_element_type=f32,
             ).reshape(8, H, E)
-        line = halves[h][4]
-        for d in (2, 1, 3):
-            k = lax.rem(line + d, XS)
-            put(out, k, gi[pl.ds(k * XS, XS)].reshape(XS * H, E))
-            ca_copy(h, k, line).start()
+
+        def ca_send(n, _, h=h):
+            gi, out, me, line = back[h][0], back[h][1], halves[h][2], halves[h][4]
+            i = lax.rem(me + 1 + lax.div(n, 3), XS)
+            k = lax.rem(line + 1 + lax.rem(n, 3), XS)
+            put(out, k * XS + i, gi[k * XS + i])
+            ca_copy(h, i, k, line).start()
+            return 0
+
+        lax.fori_loop(0, 3 * XS, ca_send, 0)
+
+    def tile_text(b):
+        w = w_ref.at[pl.ds(pl.multiple_of(b * (4 * R), 4 * R), 4 * R)]
+        total = jnp.dot(w[:, 0:half], unit_0[...].reshape(half, E), preferred_element_type=f32)
+        total = total + jnp.dot(w[:, half:], unit_1[...].reshape(half, E), preferred_element_type=f32)
+        gt[pl.ds(b * 4, 4)] = total.reshape(4, R, E)
+
+    def gt_copy(b):
+        return copy(
+            gt.at[pl.ds(oc * ZS + b * 4, 4)], gt_sib.at[pl.ds(b * 4, 4)], gt_ss.at[b], gt_rs.at[b], sibling
+        )
+
+    def tile_other(b, _):
+        tile_text(2 * oc + b)
+        gt_copy(b).start()
+        return 0
+
+    def tile_own(b, _):
+        tile_text(2 * c + b)
+        return 0
+
+    lax.fori_loop(0, 2, tile_other, 0)
+    lax.fori_loop(0, 2, tile_own, 0)
+    gt_copy(0).wait_recv()
+    gt_copy(1).wait_recv()
+
+    def c_t_copy(zz, slot):
+        return copy(c_t_out.at[zz], c_t_in.at[slot], c_t_ss.at[zz], c_t_rs.at[slot], device(ylo, zz, c, t))
+
+    def c_t_send(j, _):
+        zz = z_peer(j)
+        put(c_t_out, zz, gt[c * ZS + zz] + gt_sib[zz])
+        c_t_copy(zz, z).start()
+        return 0
+
+    lax.fori_loop(1, ZS, c_t_send, 0)
 
     for h in (0, 1):
         gi, into, part, out = back[h][0], back[h][2], back[h][3], back[h][4]
         me, line = halves[h][2], halves[h][4]
-        total = gi[pl.ds(line * XS, XS)].reshape(XS * H, E)
-        for d in (1, 3, 2):
-            k = lax.rem(line + d, XS)
-            ca_copy(h, k, k).wait_recv()
-            total = total + decode(into, k)
-        part[...] = total.reshape(XS, H, E)
-        for d in (2, 1, 3):
-            k = lax.rem(me + d, XS)
-            put(out, k, part[k])
-            cb_copy(h, k, me).start()
+        for e in (1, 2, 3, 0):
+            i = lax.rem(me + e, XS)
+            total = gi[line * XS + i]
+            for d in (1, 3, 2):
+                k = lax.rem(line + d, XS)
+                ca_copy(h, i, k, k).wait_recv()
+                total = total + take(into, k * XS + i, H)
+            if e:
+                put(out, i, total)
+                cb_copy(h, i, me).start()
+            else:
+                part[...] = total
 
     def c_i_take(h):
         into, part, me = back[h][5], back[h][3], halves[h][2]
-        total = part[me]
+        total = part[...]
         for d in (1, 3, 2):
             k = lax.rem(me + d, XS)
             cb_copy(h, k, k).wait_recv()
-            total = total + decode(into, k)
+            total = total + take(into, k, H)
         return total
 
     def c_t_take(j, total):
         zz = z_peer(ZS - j)
         c_t_copy(zz, zz).wait_recv()
-        return total + decode(c_t_in, zz)
+        return total + take(c_t_in, zz, R)
 
     def d_copy(grad, ss, rs, k, slot):
         return copy(grad.at[slot], grad.at[slot], ss.at[k], rs.at[slot], (dp, k))
@@ -412,27 +454,27 @@
     e_t = (g_t, sib_t, e_t_out, e_t_in, e_t_ss, e_t_rs)
     d_take(grad_i, d_i_ss, d_i_rs)
     weight_grad(grad_i, fi_ref, g_i, 2)
-    g_i_copy = copy(g_i.at[oc], sib_i, one_ss.at[2], one_rs.at[2], sibling)
+    g_i_copy = copy(g_i.at[oc], sib_i, one_ss.at[1], one_rs.at[1], sibling)
     g_i_copy.start()
     g_i_copy.wait_recv()
     e_send(*e_i)
     d_take(grad_t, d_t_ss, d_t_rs)
     weight_grad(grad_t, ft_ref, g_t, 3)
-    g_t_copy = copy(g_t.at[oc], sib_t, one_ss.at[3], one_rs.at[3], sibling)
+    g_t_copy = copy(g_t.at[oc], sib_t, one_ss.at[2], one_rs.at[2], sibling)
     g_t_copy.start()
     g_t_copy.wait_recv()
     e_send(*e_t)
 
-    def unpack(total, lane, width, fold):
+    def unpack(total, out, width, fold):
         rest, rows = width - 128, OUT // fold
-        out_ref[0:OUT, lane:lane + 128] = total[0:OUT, :]
+        out[:, 0:128] = total[0:OUT, :]
         for n in range(fold):
-            out_ref[n * rows:(n + 1) * rows, lane + 128:lane + width] = (
+            out[n * rows:(n + 1) * rows, 128:width] = (
                 total[OUT:OUT + rows, n * rest:(n + 1) * rest]
             )
 
-    unpack(e_take(*e_i), 0, DI, 2)
-    unpack(e_take(*e_t), 256, DT, 3)
+    unpack(e_take(*e_i), out_i, DI, 2)
+    unpack(e_take(*e_t), out_t, DT, 3)
 
     def sent_tensor(j, _):
         k = tensor_peer(j)
@@ -465,45 +507,45 @@
     for d, h in steps:
         me, line = halves[h][2], halves[h][4]
         ba_copy(h, lax.rem(me + d, XS), me).wait_send()
-        bb_copy(h, lax.rem(line + d, XS), line).wait_send()
-        ca_copy(h, lax.rem(line + d, XS), line).wait_send()
         cb_copy(h, lax.rem(me + d, XS), me).wait_send()
-    for sent in (pair_copy, gt_copy, g_i_copy, g_t_copy):
+        for i in range(XS):
+            bb_copy(h, i, lax.rem(line + d, XS), line).wait_send()
+            ca_copy(h, i, lax.rem(line + d, XS), line).wait_send()
+    for b in (0, 1):
+        gt_copy(b).wait_send()
+    for sent in (pair_copy, g_i_copy, g_t_copy):
         sent.wait_send()
 
 
 def on_device(image_features, text_features, image_weight, text_weight, image_pair, temp_index, bias_index):
-    vmem = pl.BlockSpec(memory_space=pltpu.VMEM)
-    smem = pl.BlockSpec(memory_space=pltpu.SMEM)
-    hbm = pl.BlockSpec(memory_space=pl.ANY)
+    hbm = pl.BlockSpec(memory_space=pltpu.HBM)
     dma = pltpu.SemaphoreType.DMA
-    i16 = jnp.int16
     V = pltpu.VMEM
-    acc = pl.pallas_call(
+    i16, i32 = jnp.int16, jnp.int32
+    wire = lambda count, rows: V((count, G * rows + 16, 128), i16)
+    scratch = (
+        [pltpu.SMEM((1,), i32)] * 2
+        + [V((DI, 256), bf16), V((DT, 256), bf16), V((DI, E), bf16), V((DT, E), bf16)]
+        + [V((TS, R, E), f32)] * 2 + [wire(TS, R)] * 4
+        + [V((R, E), f32)] * 2 + [V((R, 1), f32)] * 2
+        + [V((PS, H, E), bf16)] * 2 + [V((PS, R, E), bf16)]
+        + [V((8, 256), i32)] * 2 + [V((8, PS * R), i32)]
+        + [V((PS * R, PS * R), bf16)] + [V((PS, H, E), f32)] * 2 + [V((PS, R, E), f32), V((ZS, R, E), f32)]
+        + [wire(PS, H)] * 4 + [V((H, E), f32)] * 2 + [wire(XS, H)] * 4 + [wire(ZS, R)] * 2
+        + [V((TS, R, E), bf16)] * 2
+        + [V((2, PS, ROWS_I, 128), f32), V((2, PS, ROWS_T, 128), f32)]
+        + [V((PS, ROWS_I, 128), f32), V((PS, ROWS_T, 128), f32)]
+        + [V((PS, ROWS_I, 128), bf16)] * 2 + [V((PS, ROWS_T, 128), bf16)] * 2
+        + [dma((7,))] + [dma((TS,))] * 4 + [dma((2 * XS,))] * 2 + [dma((2 * PS,))] * 2 + [dma((ZS,))] * 4
+        + [dma((2 * PS,))] * 2 + [dma((2 * XS,))] * 2 + [dma((2,))] * 2 + [dma((ZS,))] * 2
+        + [dma((TS,))] * 4 + [dma((PS,))] * 4 + [dma((3,))] * 2
+    )
+    grad_image, grad_text = pl.pallas_call(
         kernel,
-        out_shape=jax.ShapeDtypeStruct((40, 512), f32),
-        in_specs=[smem, smem] + [hbm] * 5,
-        out_specs=vmem,
-        scratch_shapes=[
-            V((DI, 256), bf16), V((DT, 256), bf16), V((DI, E), bf16), V((DT, E), bf16),
-            V((TS, R, E), f32), V((TS, R, E), f32),
-            V((TS, R, WIRE), i16), V((TS, R, WIRE), i16), V((TS, R, WIRE), i16), V((TS, R, WIRE), i16),
-            V((R, E), f32), V((R, E), f32), V((R, 1), f32), V((R, 1), f32),
-            V((PS, H, E), bf16), V((PS, H, E), bf16), V((PS, R, E), bf16),
-            V((8, 256), jnp.int32), V((8, 256), jnp.int32), V((8, PS * R), jnp.int32),
-            V((PS * R, PS * R), bf16), V((PS, H, E), f32), V((PS, H, E), f32), V((PS, R, E), f32), V((ZS, R, E), f32),
-        ]
-        + [V((XS, XS * H, WIRE), i16)] * 4
-        + [V((XS, H, E), f32)] * 2 + [V((XS, H, WIRE), i16)] * 4 + [V((ZS, R, WIRE), i16)] * 2
-        + [
-            V((TS, R, E), bf16), V((TS, R, E), bf16),
-            V((2, PS, ROWS_I, 128), f32), V((2, PS, ROWS_T, 128), f32),
-            V((PS, ROWS_I, 128), f32), V((PS, ROWS_T, 128), f32),
-            V((PS, ROWS_I, 128), bf16), V((PS, ROWS_I, 128), bf16),
-            V((PS, ROWS_T, 128), bf16), V((PS, ROWS_T, 128), bf16),
-        ]
-        + [dma((5,))] + [dma((TS,))] * 4 + [dma((2 * XS,))] * 4 + [dma((ZS,))] * 4
-        + [dma((2 * XS,))] * 4 + [dma((ZS,))] * 2 + [dma((TS,))] * 4 + [dma((PS,))] * 4 + [dma((4,))] * 2,
+        out_shape=[jax.ShapeDtypeStruct((OUT, DI), f32), jax.ShapeDtypeStruct((OUT, DT), f32)],
+        in_specs=[hbm] * 7,
+        out_specs=[pl.BlockSpec(memory_space=pltpu.VMEM)] * 2,
+        scratch_shapes=scratch,
         compiler_params=pltpu.CompilerParams(
             collective_id=0, has_side_effects=True, vmem_limit_bytes=56 * 2**20
         ),
@@ -512,7 +554,7 @@
         temp_index.reshape(1), bias_index.reshape(1), image_pair.reshape(1, 256),
         image_features.T, text_features.T, image_weight, text_weight,
     )
-    return acc[0:OUT, 0:DI].T, acc[0:OUT, 256:256 + DT].T
+    return grad_image.T, grad_text.T
 
 
 def solution(mesh):

time: 94 us -> 91.9 us (0.978)
  Pallas kernels: 89.9 us -> 87.8 us
    transpose x2 -> x0, local copies, waits for them, and re-layouts: 2.08 us -> none  [on_device(): return (acc[0:OUT, 0:DI].T, acc[0:OUT, 256:256 + DT].T)]
    pallas_call x1, Pallas kernels: 89.9 us -> 87.8 us  [on_device(): pl.pallas_call(kernel, out_shape=[jax.ShapeDtypeStruct((OUT, DI), f32), j...]
    unnamed x2 -> x4, local copies, waits for them, and re-layouts: 0.01 us -> 2.03 us
where the time goes in v3:
time: 91.9 us; the launch traced here: 91.8 us
  Pallas kernels  87.8 us (96%)
  local copies, waits for them, and re-layouts  2.03 us (2%)
  between operations  1.94 us (2%)
    pallas_call x1, Pallas kernels, on_device(): pl.pallas_call(kernel, out_shape=[jax.ShapeDtypeStruct((OUT, DI), f32), j...  87.8 us
    unnamed x4, local copies, waits for them, and re-layouts  2.03 us

profile of v3, /device:TPU:1, one launch (start us, length us, event | category | flops | bytes accessed | tf_op | source)
XLA Modules:
  0.0 91.8 jit_solution(3196633053553699693)
XLA Ops:
  1.9 87.8 %pair_loss_grads.1 = (f32[36,176]{1,0:T(8,128)}, f32[36,144]{1,0:T(8,128)}) custom-call(s32[1]{0:T(128)} %bitcast.7.temp_hbm, s32[1]{0:T(128)} %bitcast.8.bias_hbm, s32[1,256]{1,0:T(1,128)} %bitcast.13, bf16[176,256]{1,0:T(8,128)(2,1)} %bitcast.9, bf16[144,256]{1,0:T(8,128)(2,1)} %bitcast.10, bf16[176,1152]{1,0:T(8,128)(2,1)} %wi_hbm.1, bf16[144,1152]{1,0:T(8,128)(2,1)} %wt_hbm.1), custom_call_target="tpu_custom_call" | custom-call | tf_op jit(solution)/shard_map/pair_loss_grads/pallas_call | solution.py:543
  89.7 0.0 copy-start
  89.7 1.4 %copy.13 = f32[176,36]{0,1:T(8,128)} copy(f32[176,36]{0,1:T(8,128)} %bitcast.12) | data formatting | bytes 50688
  91.1 0.0 copy-done
  91.1 0.6 copy.14
Async XLA Ops:
  89.7 1.4 %copy-start = (f32[36,144]{1,0:T(8,128)S(1)}, f32[36,144]{1,0:T(8,128)}, u32[]{:S(2)}) copy-start(f32[36,144]{1,0:T(8,128)} %get-tuple-element.5) | copy-start | bytes 62212

commit v4 on v3

--- a/solution.py
+++ b/solution.py
@@ -24,21 +24,22 @@
 bf16 = jnp.bfloat16
 
 
-def put(wire, k, x):
-    n = x.shape[0]
+def put(wire, k, x, n):
     m = jnp.max(jnp.abs(x), axis=1, keepdims=True)
     hi = jnp.floor(m)
     lo = jnp.floor((m - hi) * LEVELS) + 1.0
     q = jnp.round(x * (LEVELS / (hi + lo * (1.0 / LEVELS)))).astype(jnp.int32).astype(jnp.int16)
-    for g in range(G):
-        wire[k, g * n:(g + 1) * n, :] = q[:, g * 128:(g + 1) * 128]
-    diagonal = lax.broadcasted_iota(jnp.int32, (n, 128), 0) == lax.broadcasted_iota(jnp.int32, (n, 128), 1)
-    hi = jnp.sum(jnp.where(diagonal, hi, 0.0), axis=0, keepdims=True)
-    lo = jnp.sum(jnp.where(diagonal, lo, 0.0), axis=0, keepdims=True)
-    row = lax.broadcasted_iota(jnp.int32, (16, 128), 0)
-    wire[k, G * n:G * n + 16, :] = (
-        jnp.where(row == 0, hi, jnp.where(row == 1, lo, 0.0)).astype(jnp.int32).astype(jnp.int16)
-    )
+    for i in range(x.shape[0] // n):
+        rows = slice(i * n, (i + 1) * n)
+        for g in range(G):
+            wire[k + i, g * n:(g + 1) * n, :] = q[rows, g * 128:(g + 1) * 128]
+        diagonal = lax.broadcasted_iota(jnp.int32, (n, 128), 0) == lax.broadcasted_iota(jnp.int32, (n, 128), 1)
+        his = jnp.sum(jnp.where(diagonal, hi[rows], 0.0), axis=0, keepdims=True)
+        los = jnp.sum(jnp.where(diagonal, lo[rows], 0.0), axis=0, keepdims=True)
+        row = lax.broadcasted_iota(jnp.int32, (16, 128), 0)
+        wire[k + i, G * n:G * n + 16, :] = (
+            jnp.where(row == 0, his, jnp.where(row == 1, los, 0.0)).astype(jnp.int32).astype(jnp.int16)
+        )
 
 
 def take(wire, k, n):
@@ -115,12 +116,16 @@
         j = lax.rem(j * 5, TS)
         return lax.rem(yhi + lax.div(j, XS), 2) * XS + lax.rem(x + lax.rem(j, XS), XS)
 
+    def z_step(n):
+        m = lax.div(n + 1, 2)
+        return lax.rem(4 + m * (1 - 2 * lax.rem(n, 2)) + ZS, ZS)
+
     def z_peer(j):
-        return lax.rem(z + j * 3, ZS)
+        return lax.rem(z + z_step(j - 1), ZS)
 
     def column_peer(j):
-        j = lax.rem(j * 7, PS)
-        return lax.rem(ylo + lax.div(j, ZS), 2) * ZS + lax.rem(z + lax.rem(j, ZS), ZS)
+        n = j - 1
+        return lax.rem(ylo + 1 - lax.rem(n, 2), 2) * ZS + lax.rem(z + z_step(lax.div(n, 2)), ZS)
 
     def copy(src, dst, ssem, rsem, dev):
         return pltpu.make_async_remote_copy(
@@ -163,12 +168,10 @@
         return copy(wire_out.at[k], wire_in.at[slot], ss.at[k], rs.at[slot], (dp, k))
 
     def a_send(part, wire_out, wire_in, ss, rs):
-        def step(j, _):
-            k = tensor_peer(j)
-            put(wire_out, k, part[k])
-            a_copy(wire_out, wire_in, ss, rs, k, t).start()
-            return 0
-        lax.fori_loop(1, TS, step, 0)
+        for hi in (1 - yhi, yhi):
+            put(wire_out, hi * XS, part[pl.ds(hi * XS, XS)].reshape(XS * R, E), R)
+            for d in (2, 1, 3) if hi is yhi else (2, 1, 3, 0):
+                a_copy(wire_out, wire_in, ss, rs, hi * XS + lax.rem(x + d, XS), t).start()
 
     def a_take(part, wire_out, wire_in, ss, rs):
         def step(j, total):
@@ -262,7 +265,7 @@
             bb_send(h, k)
 
     def b_t_take(j, _):
-        zz = z_peer(ZS - j)
+        zz = z_peer(j)
         b_t_copy(zz, zz).wait_recv()
         relay(c, zz).start()
         return 0
@@ -321,15 +324,15 @@
                 preferred_element_type=f32,
             ).reshape(8, H, E)
 
-        def ca_send(n, _, h=h):
-            gi, out, me, line = back[h][0], back[h][1], halves[h][2], halves[h][4]
-            i = lax.rem(me + 1 + lax.div(n, 3), XS)
-            k = lax.rem(line + 1 + lax.rem(n, 3), XS)
-            put(out, k * XS + i, gi[k * XS + i])
-            ca_copy(h, i, k, line).start()
-            return 0
-
-        lax.fori_loop(0, 3 * XS, ca_send, 0)
+        out, me, line = back[h][1], halves[h][2], halves[h][4]
+        for d in (2, 1, 3):
+            k = lax.rem(line + d, XS)
+            put(out, k * XS, gi[pl.ds(k * XS, XS)].reshape(XS * H, E), H)
+            for e in (2, 1, 3):
+                ca_copy(h, lax.rem(me + e, XS), k, line).start()
+    for d, h in steps:
+        me, line = halves[h][2], halves[h][4]
+        ca_copy(h, me, lax.rem(line + d, XS), line).start()
 
     def tile_text(b):
         w = w_ref.at[pl.ds(pl.multiple_of(b * (4 * R), 4 * R), 4 * R)]
@@ -347,25 +350,25 @@
         gt_copy(b).start()
         return 0
 
+    def c_t_copy(zz, slot):
+        return copy(c_t_out.at[zz], c_t_in.at[slot], c_t_ss.at[zz], c_t_rs.at[slot], device(ylo, zz, c, t))
+
     def tile_own(b, _):
         tile_text(2 * c + b)
+        gt_copy(b).wait_recv()
+        rows = gt[pl.ds(c * ZS + b * 4, 4)] + gt_sib[pl.ds(b * 4, 4)]
+        gt[pl.ds(c * ZS + b * 4, 4)] = rows
+        put(c_t_out, b * 4, rows.reshape(4 * R, E), R)
+        for n in range(4):
+            zz = b * 4 + n
+
+            @pl.when(zz != z)
+            def _(zz=zz):
+                c_t_copy(zz, z).start()
         return 0
 
     lax.fori_loop(0, 2, tile_other, 0)
     lax.fori_loop(0, 2, tile_own, 0)
-    gt_copy(0).wait_recv()
-    gt_copy(1).wait_recv()
-
-    def c_t_copy(zz, slot):
-        return copy(c_t_out.at[zz], c_t_in.at[slot], c_t_ss.at[zz], c_t_rs.at[slot], device(ylo, zz, c, t))
-
-    def c_t_send(j, _):
-        zz = z_peer(j)
-        put(c_t_out, zz, gt[c * ZS + zz] + gt_sib[zz])
-        c_t_copy(zz, z).start()
-        return 0
-
-    lax.fori_loop(1, ZS, c_t_send, 0)
 
     for h in (0, 1):
         gi, into, part, out = back[h][0], back[h][2], back[h][3], back[h][4]
@@ -378,7 +381,7 @@
                 ca_copy(h, i, k, k).wait_recv()
                 total = total + take(into, k * XS + i, H)
             if e:
-                put(out, i, total)
+                put(out, i, total, H)
                 cb_copy(h, i, me).start()
             else:
                 part[...] = total
@@ -393,7 +396,7 @@
         return total
 
     def c_t_take(j, total):
-        zz = z_peer(ZS - j)
+        zz = z_peer(j)
         c_t_copy(zz, zz).wait_recv()
         return total + take(c_t_in, zz, R)
 
@@ -416,7 +419,7 @@
     total = jnp.concatenate([c_i_take(0), c_i_take(1)], axis=0)
     grad_i[t] = back_rows(dir_i[...], norm_i[...], total)
     d_send(grad_i, d_i_ss, d_i_rs)
-    total = lax.fori_loop(1, ZS, c_t_take, gt[c * ZS + z] + gt_sib[z])
+    total = lax.fori_loop(1, ZS, c_t_take, gt[c * ZS + z])
     grad_t[t] = back_rows(dir_t[...], norm_t[...], total)
     d_send(grad_t, d_t_ss, d_t_rs)
 
@@ -445,7 +448,7 @@
 
     def e_take(packed, sib, out, into, ss, rs):
         def step(j, total):
-            k = column_peer(PS - j)
+            k = column_peer(j)
             e_copy(out, into, ss, rs, k, k).wait_recv()
             return total + into[k].astype(f32)
         return lax.fori_loop(1, PS, step, packed[c, q] + sib[q])
@@ -547,7 +550,7 @@
         out_specs=[pl.BlockSpec(memory_space=pltpu.VMEM)] * 2,
         scratch_shapes=scratch,
         compiler_params=pltpu.CompilerParams(
-            collective_id=0, has_side_effects=True, vmem_limit_bytes=56 * 2**20
+            collective_id=0, has_side_effects=True, vmem_limit_bytes=56430000
         ),
         name="pair_loss_grads",
     )(

time: 91.9 us -> 92.5 us (level)
  no operation moved by 1% of the time
where the time goes in v4:
time: 92.5 us; the launch traced here: 92.3 us
  Pallas kernels  88.5 us (96%)
  between operations  1.94 us (2%)
  local copies, waits for them, and re-layouts  1.91 us (2%)
    pallas_call x1, Pallas kernels, on_device(): pl.pallas_call(kernel, out_shape=[jax.ShapeDtypeStruct((OUT, DI), f32), j...  88.5 us
    unnamed x4, local copies, waits for them, and re-layouts  1.91 us

profile of v4, /device:TPU:1, one launch (start us, length us, event | category | flops | bytes accessed | tf_op | source)
XLA Modules:
  0.0 92.3 jit_solution(7029050711566951133)
XLA Ops:
  1.9 0.0 copy-start
  1.9 0.7 copy-done
  2.6 88.5 %pair_loss_grads.1 = (f32[36,176]{1,0:T(8,128)S(1)}, f32[36,144]{1,0:T(8,128)S(1)}) custom-call(s32[1]{0:T(128)} %bitcast.7.temp_hbm, s32[1]{0:T(128)} %bitcast.8.bias_hbm, s32[1,256]{1,0:T(1,128)S(1)} %bitcast.11, bf16[176,256]{1,0:T(8,128)(2,1)} %bitcast.12, bf16[144,256]{1,0:T(8,128)(2,1)} %bitcast.13, bf16[176,1152]{1,0:T(8,128)(2,1)} %wi_hbm.1, ...), custom_call_target="tpu_custom_call" | custom-call | tf_op jit(solution)/shard_map/pair_loss_grads/pallas_call | solution.py:546
  91.1 0.6 copy.13
  91.7 0.6 copy.14
Async XLA Ops:
  1.9 0.7 copy-start

commit v5 on v4

--- a/solution.py
+++ b/solution.py
@@ -69,10 +69,10 @@
     part_i, part_t, a_i_out, a_i_in, a_t_out, a_t_in,
     dir_i, dir_t, norm_i, norm_t, unit_0, unit_1, all_t, pair_out, pair_in, target_ref,
     w_ref, gi_0, gi_1, gt, gt_sib, ca_out_0, ca_in_0, ca_out_1, ca_in_1,
-    half_0, half_1, cb_out_0, cb_in_0, cb_out_1, cb_in_1, c_t_out, c_t_in,
+    half_0, half_1, cb_out_0, cb_in_0, cb_out_1, cb_in_1, co_out_0, co_in_0, co_out_1, co_in_1, c_t_out, c_t_in,
     grad_i, grad_t, g_i, g_t, sib_i, sib_t, e_i_out, e_i_in, e_t_out, e_t_in,
     load_s, a_i_ss, a_i_rs, a_t_ss, a_t_rs, ba_ss, ba_rs, bb_ss, bb_rs, b_t_ss, b_t_rs, relay_ss, relay_rs,
-    ca_ss, ca_rs, cb_ss, cb_rs, gt_ss, gt_rs, c_t_ss, c_t_rs, d_i_ss, d_i_rs, d_t_ss, d_t_rs,
+    ca_ss, ca_rs, co_ss, co_rs, cb_ss, cb_rs, gt_ss, gt_rs, c_t_ss, c_t_rs, d_i_ss, d_i_rs, d_t_ss, d_t_rs,
     e_i_ss, e_i_rs, e_t_ss, e_t_rs, one_ss, one_rs,
 ):
     loads = [
@@ -288,73 +288,69 @@
     shift = -0.5 * bias_ref[0].astype(f32)
     half = PS * H
 
-    def tile_weights(b, _):
-        rows = all_t[pl.ds(b * 4, 4)].reshape(4 * R, E)
-        for h, unit in ((0, unit_0), (1, unit_1)):
-            logits = scale * lax.dot_general(
-                rows, unit[...].reshape(half, E), (((1,), (1,)), ((), ())), preferred_element_type=f32
-            ) + shift
-            index = lax.broadcasted_iota(jnp.int32, (4 * R, half), 0) + b * (4 * R)
-            sign = jnp.where(index == target_ref[0:1, h * half:(h + 1) * half], f32(1.0), f32(-1.0))
-            w = (-scale * sign * jax.nn.sigmoid(-sign * logits)).astype(bf16)
-            w_ref[pl.ds(pl.multiple_of(b * (4 * R), 4 * R), 4 * R), h * half:(h + 1) * half] = w
-        return 0
-
-    lax.fori_loop(0, 4, tile_weights, 0)
-
-    back = ((gi_0, ca_out_0, ca_in_0, half_0, cb_out_0, cb_in_0), (gi_1, ca_out_1, ca_in_1, half_1, cb_out_1, cb_in_1))
-
-    def ca_copy(h, i, k, slot):
+    for h, unit in ((0, unit_0), (1, unit_1)):
+        logits = scale * lax.dot_general(
+            all_t[...].reshape(PS * R, E), unit[...].reshape(half, E), (((1,), (1,)), ((), ())),
+            preferred_element_type=f32,
+        ) + shift
+        index = lax.broadcasted_iota(jnp.int32, (PS * R, half), 0)
+        sign = jnp.where(index == target_ref[0:1, h * half:(h + 1) * half], f32(1.0), f32(-1.0))
+        w_ref[:, h * half:(h + 1) * half] = (-scale * sign * jax.nn.sigmoid(-sign * logits)).astype(bf16)
+
+    back = ((gi_0, ca_out_0, ca_in_0, half_0, cb_out_0, cb_in_0, co_out_0, co_in_0), (gi_1, ca_out_1, ca_in_1, half_1, cb_out_1, cb_in_1, co_out_1, co_in_1))
+
+    def ca_copy(h, k, slot):
         out, into = back[h][1], back[h][2]
         return copy(
-            out.at[k * XS + i], into.at[slot * XS + i],
-            ca_ss.at[h * PS + k * XS + i], ca_rs.at[h * PS + slot * XS + i], halves[h][3](k),
+            out.at[k], into.at[slot], ca_ss.at[h * XS + k], ca_rs.at[h * XS + slot], halves[h][3](k)
         )
 
-    def cb_copy(h, k, slot):
+    def co_copy(h, k, slot):
+        out, into = back[h][6], back[h][7]
+        return copy(
+            out.at[k], into.at[slot], co_ss.at[h * XS + k], co_rs.at[h * XS + slot], halves[h][3](k)
+        )
+
+    def others(gi, h, k):
+        return jnp.concatenate([gi[k * XS + lax.rem(halves[h][2] + e, XS)] for e in (2, 1, 3)], axis=0)
+
+    def cb_copy(h, n, k, slot):
         out, into = back[h][4], back[h][5]
-        return copy(out.at[k], into.at[slot], cb_ss.at[h * XS + k], cb_rs.at[h * XS + slot], halves[h][1](k))
+        return copy(out.at[n], into.at[slot], cb_ss.at[h * XS + n], cb_rs.at[h * XS + slot], halves[h][1](k))
 
     for h in (0, 1):
         gi = back[h][0]
-        for b in range(2):
-            lane = h * half + b * 128
-            gi[8 * b:8 * b + 8] = lax.dot_general(
-                w_ref[:, lane:lane + 128], all_t[...].reshape(PS * R, E), (((0,), (0,)), ((), ())),
-                preferred_element_type=f32,
-            ).reshape(8, H, E)
-
+        gi[...] = lax.dot_general(
+            w_ref[:, h * half:(h + 1) * half], all_t[...].reshape(PS * R, E), (((0,), (0,)), ((), ())),
+            preferred_element_type=f32,
+        ).reshape(PS, H, E)
         out, me, line = back[h][1], halves[h][2], halves[h][4]
         for d in (2, 1, 3):
             k = lax.rem(line + d, XS)
-            put(out, k * XS, gi[pl.ds(k * XS, XS)].reshape(XS * H, E), H)
-            for e in (2, 1, 3):
-                ca_copy(h, lax.rem(me + e, XS), k, line).start()
-    for d, h in steps:
-        me, line = halves[h][2], halves[h][4]
-        ca_copy(h, me, lax.rem(line + d, XS), line).start()
-
-    def tile_text(b):
-        w = w_ref.at[pl.ds(pl.multiple_of(b * (4 * R), 4 * R), 4 * R)]
+            put(out, k, others(gi, h, k), 3 * H)
+            ca_copy(h, k, line).start()
+    for h in (0, 1):
+        gi, own, me, line = back[h][0], back[h][6], halves[h][2], halves[h][4]
+        for d in (2, 1, 3):
+            k = lax.rem(line + d, XS)
+            put(own, k, gi[k * XS + me], H)
+            co_copy(h, k, line).start()
+
+    def tile_text(cc):
+        w = w_ref.at[pl.ds(pl.multiple_of(cc * (ZS * R), ZS * R), ZS * R)]
         total = jnp.dot(w[:, 0:half], unit_0[...].reshape(half, E), preferred_element_type=f32)
         total = total + jnp.dot(w[:, half:], unit_1[...].reshape(half, E), preferred_element_type=f32)
-        gt[pl.ds(b * 4, 4)] = total.reshape(4, R, E)
+        gt[pl.ds(cc * ZS, ZS)] = total.reshape(ZS, R, E)
 
     def gt_copy(b):
         return copy(
             gt.at[pl.ds(oc * ZS + b * 4, 4)], gt_sib.at[pl.ds(b * 4, 4)], gt_ss.at[b], gt_rs.at[b], sibling
         )
 
-    def tile_other(b, _):
-        tile_text(2 * oc + b)
-        gt_copy(b).start()
-        return 0
-
     def c_t_copy(zz, slot):
         return copy(c_t_out.at[zz], c_t_in.at[slot], c_t_ss.at[zz], c_t_rs.at[slot], device(ylo, zz, c, t))
 
     def tile_own(b, _):
-        tile_text(2 * c + b)
         gt_copy(b).wait_recv()
         rows = gt[pl.ds(c * ZS + b * 4, 4)] + gt_sib[pl.ds(b * 4, 4)]
         gt[pl.ds(c * ZS + b * 4, 4)] = rows
@@ -367,31 +363,39 @@
                 c_t_copy(zz, z).start()
         return 0
 
-    lax.fori_loop(0, 2, tile_other, 0)
+    tile_text(oc)
+    gt_copy(0).start()
+    gt_copy(1).start()
+    tile_text(c)
     lax.fori_loop(0, 2, tile_own, 0)
 
     for h in (0, 1):
         gi, into, part, out = back[h][0], back[h][2], back[h][3], back[h][4]
         me, line = halves[h][2], halves[h][4]
-        for e in (1, 2, 3, 0):
-            i = lax.rem(me + e, XS)
-            total = gi[line * XS + i]
-            for d in (1, 3, 2):
-                k = lax.rem(line + d, XS)
-                ca_copy(h, i, k, k).wait_recv()
-                total = total + take(into, k * XS + i, H)
-            if e:
-                put(out, i, total, H)
-                cb_copy(h, i, me).start()
-            else:
-                part[...] = total
+        total = others(gi, h, line)
+        for d in (1, 3, 2):
+            k = lax.rem(line + d, XS)
+            ca_copy(h, k, k).wait_recv()
+            total = total + take(into, k, 3 * H)
+        put(out, 0, total, H)
+        for n, e in enumerate((2, 1, 3)):
+            cb_copy(h, n, lax.rem(me + e, XS), me).start()
+    for h in (0, 1):
+        gi, own, part = back[h][0], back[h][7], back[h][3]
+        me, line = halves[h][2], halves[h][4]
+        total = gi[line * XS + me]
+        for d in (1, 3, 2):
+            k = lax.rem(line + d, XS)
+            co_copy(h, k, k).wait_recv()
+            total = total + take(own, k, H)
+        part[...] = total
 
     def c_i_take(h):
         into, part, me = back[h][5], back[h][3], halves[h][2]
         total = part[...]
         for d in (1, 3, 2):
             k = lax.rem(me + d, XS)
-            cb_copy(h, k, k).wait_recv()
+            cb_copy(h, 0, k, k).wait_recv()
             total = total + take(into, k, H)
         return total
 
@@ -510,10 +514,13 @@
     for d, h in steps:
         me, line = halves[h][2], halves[h][4]
         ba_copy(h, lax.rem(me + d, XS), me).wait_send()
-        cb_copy(h, lax.rem(me + d, XS), me).wait_send()
+        ca_copy(h, lax.rem(line + d, XS), line).wait_send()
+        co_copy(h, lax.rem(line + d, XS), line).wait_send()
         for i in range(XS):
             bb_copy(h, i, lax.rem(line + d, XS), line).wait_send()
-            ca_copy(h, i, lax.rem(line + d, XS), line).wait_send()
+    for h in (0, 1):
+        for n, e in enumerate((2, 1, 3)):
+            cb_copy(h, n, lax.rem(halves[h][2] + e, XS), halves[h][2]).wait_send()
     for b in (0, 1):
         gt_copy(b).wait_send()
     for sent in (pair_copy, g_i_copy, g_t_copy):
@@ -534,13 +541,13 @@
         + [V((PS, H, E), bf16)] * 2 + [V((PS, R, E), bf16)]
         + [V((8, 256), i32)] * 2 + [V((8, PS * R), i32)]
         + [V((PS * R, PS * R), bf16)] + [V((PS, H, E), f32)] * 2 + [V((PS, R, E), f32), V((ZS, R, E), f32)]
-        + [wire(PS, H)] * 4 + [V((H, E), f32)] * 2 + [wire(XS, H)] * 4 + [wire(ZS, R)] * 2
+        + [wire(XS, 3 * H)] * 4 + [V((H, E), f32)] * 2 + [wire(XS, H)] * 8 + [wire(ZS, R)] * 2
         + [V((TS, R, E), bf16)] * 2
         + [V((2, PS, ROWS_I, 128), f32), V((2, PS, ROWS_T, 128), f32)]
         + [V((PS, ROWS_I, 128), f32), V((PS, ROWS_T, 128), f32)]
         + [V((PS, ROWS_I, 128), bf16)] * 2 + [V((PS, ROWS_T, 128), bf16)] * 2
         + [dma((7,))] + [dma((TS,))] * 4 + [dma((2 * XS,))] * 2 + [dma((2 * PS,))] * 2 + [dma((ZS,))] * 4
-        + [dma((2 * PS,))] * 2 + [dma((2 * XS,))] * 2 + [dma((2,))] * 2 + [dma((ZS,))] * 2
+        + [dma((2 * XS,))] * 6 + [dma((2,))] * 2 + [dma((ZS,))] * 2
         + [dma((TS,))] * 4 + [dma((PS,))] * 4 + [dma((3,))] * 2
     )
     grad_image, grad_text = pl.pallas_call(

time: 92.5 us -> 90 us (0.973)
  Pallas kernels: 88.5 us -> 86 us
    pallas_call x1, Pallas kernels: 88.5 us -> 86 us  [on_device(): pl.pallas_call(kernel, out_shape=[jax.ShapeDtypeStruct((OUT, DI), f32), j...]
where the time goes in v5:
time: 90 us; the launch traced here: 89.8 us
  Pallas kernels  86 us (96%)
  between operations  1.94 us (2%)
  local copies, waits for them, and re-layouts  1.91 us (2%)
    pallas_call x1, Pallas kernels, on_device(): pl.pallas_call(kernel, out_shape=[jax.ShapeDtypeStruct((OUT, DI), f32), j...  86 us
    unnamed x4, local copies, waits for them, and re-layouts  1.91 us

profile of v5, /device:TPU:1, one launch (start us, length us, event | category | flops | bytes accessed | tf_op | source)
XLA Modules:
  0.0 89.8 jit_solution(7459408688478789549)
XLA Ops:
  1.9 0.0 copy-start
  1.9 0.7 copy-done
  2.6 86.0 %pair_loss_grads.1 = (f32[36,176]{1,0:T(8,128)S(1)}, f32[36,144]{1,0:T(8,128)S(1)}) custom-call(s32[1]{0:T(128)} %bitcast.7.temp_hbm, s32[1]{0:T(128)} %bitcast.8.bias_hbm, s32[1,256]{1,0:T(1,128)S(1)} %bitcast.11, bf16[176,256]{1,0:T(8,128)(2,1)} %bitcast.12, bf16[144,256]{1,0:T(8,128)(2,1)} %bitcast.13, bf16[176,1152]{1,0:T(8,128)(2,1)} %wi_hbm.1, ...), custom_call_target="tpu_custom_call" | custom-call | tf_op jit(solution)/shard_map/pair_loss_grads/pallas_call | solution.py:553
  88.6 0.6 copy.13
  89.2 0.6 copy.14
Async XLA Ops:
  1.9 0.7 copy-start

commit v6 on v5

--- a/solution.py
+++ b/solution.py
@@ -113,8 +113,13 @@
         return device(lax.div(k, ZS), lax.rem(k, ZS), c, t)
 
     def tensor_peer(j):
-        j = lax.rem(j * 5, TS)
-        return lax.rem(yhi + lax.div(j, XS), 2) * XS + lax.rem(x + lax.rem(j, XS), XS)
+        dy, dx = ((1, 2), (0, 2), (1, 1), (1, 3), (0, 1), (0, 3), (1, 0))[j - 1]
+        return lax.rem(yhi + dy, 2) * XS + lax.rem(x + dx, XS)
+
+    def tensor_steps(body, carry):
+        for j in range(1, TS):
+            carry = body(j, carry)
+        return carry
 
     def z_step(n):
         m = lax.div(n + 1, 2)
@@ -145,7 +150,7 @@
         greet(column(column_peer(j)))
         return 0
 
-    lax.fori_loop(1, TS, greet_tensor, 0)
+    tensor_steps(greet_tensor, 0)
     lax.fori_loop(1, PS, greet_column, 0)
     greet(beyond)
     greet(sibling)
@@ -178,7 +183,7 @@
             k = tensor_peer(TS - j)
             a_copy(wire_out, wire_in, ss, rs, k, k).wait_recv()
             return total + take(wire_in, k, R)
-        return lax.fori_loop(1, TS, step, part[t])
+        return tensor_steps(step, part[t])
 
     a_send(part_t, a_t_out, a_t_in, a_t_ss, a_t_rs)
     pair_copy = copy(pair_out, pair_in, one_ss.at[0], one_rs.at[0], across)
@@ -411,14 +416,14 @@
         def step(j, _):
             d_copy(grad, ss, rs, tensor_peer(j), t).start()
             return 0
-        lax.fori_loop(1, TS, step, 0)
+        tensor_steps(step, 0)
 
     def d_take(grad, ss, rs):
         def step(j, _):
             k = tensor_peer(TS - j)
             d_copy(grad, ss, rs, k, k).wait_recv()
             return 0
-        lax.fori_loop(1, TS, step, 0)
+        tensor_steps(step, 0)
 
     total = jnp.concatenate([c_i_take(0), c_i_take(1)], axis=0)
     grad_i[t] = back_rows(dir_i[...], norm_i[...], total)
@@ -480,9 +485,6 @@
                 total[OUT:OUT + rows, n * rest:(n + 1) * rest]
             )
 
-    unpack(e_take(*e_i), out_i, DI, 2)
-    unpack(e_take(*e_t), out_t, DT, 3)
-
     def sent_tensor(j, _):
         k = tensor_peer(j)
         a_copy(a_t_out, a_t_in, a_t_ss, a_t_rs, k, t).wait_send()
@@ -497,19 +499,12 @@
         c_t_copy(zz, z).wait_send()
         return 0
 
-    def sent_column(j, _):
-        k = column_peer(j)
-        e_copy(e_i_out, e_i_in, e_i_ss, e_i_rs, k, q).wait_send()
-        e_copy(e_t_out, e_t_in, e_t_ss, e_t_rs, k, q).wait_send()
-        return 0
-
     def sent_relay(zz, _):
         relay(c, zz).wait_send()
         return 0
 
-    lax.fori_loop(1, TS, sent_tensor, 0)
+    tensor_steps(sent_tensor, 0)
     lax.fori_loop(1, ZS, sent_z, 0)
-    lax.fori_loop(1, PS, sent_column, 0)
     lax.fori_loop(0, ZS, sent_relay, 0)
     for d, h in steps:
         me, line = halves[h][2], halves[h][4]
@@ -523,7 +518,19 @@
             cb_copy(h, n, lax.rem(halves[h][2] + e, XS), halves[h][2]).wait_send()
     for b in (0, 1):
         gt_copy(b).wait_send()
-    for sent in (pair_copy, g_i_copy, g_t_copy):
+    pair_copy.wait_send()
+
+    unpack(e_take(*e_i), out_i, DI, 2)
+    unpack(e_take(*e_t), out_t, DT, 3)
+
+    def sent_column(j, _):
+        k = column_peer(j)
+        e_copy(e_i_out, e_i_in, e_i_ss, e_i_rs, k, q).wait_send()
+        e_copy(e_t_out, e_t_in, e_t_ss, e_t_rs, k, q).wait_send()
+        return 0
+
+    lax.fori_loop(1, PS, sent_column, 0)
+    for sent in (g_i_copy, g_t_copy):
         sent.wait_send()
 
 

time: 90 us -> 87.7 us (0.974)
  Pallas kernels: 86 us -> 83.7 us
    pallas_call x1, Pallas kernels: 86 us -> 83.7 us  [on_device(): pl.pallas_call(kernel, out_shape=[jax.ShapeDtypeStruct((OUT, DI), f32), j...]
where the time goes in v6:
time: 87.7 us; the launch traced here: 87.5 us
  Pallas kernels  83.7 us (95%)
  between operations  1.94 us (2%)
  local copies, waits for them, and re-layouts  1.91 us (2%)
    pallas_call x1, Pallas kernels, on_device(): pl.pallas_call(kernel, out_shape=[jax.ShapeDtypeStruct((OUT, DI), f32), j...  83.7 us
    unnamed x4, local copies, waits for them, and re-layouts  1.91 us

profile of v6, /device:TPU:1, one launch (start us, length us, event | category | flops | bytes accessed | tf_op | source)
XLA Modules:
  0.0 87.5 jit_solution(14895502491614581876)
XLA Ops:
  1.9 0.0 copy-start
  1.9 0.7 copy-done
  2.6 83.7 %pair_loss_grads.1 = (f32[36,176]{1,0:T(8,128)S(1)}, f32[36,144]{1,0:T(8,128)S(1)}) custom-call(s32[1]{0:T(128)} %bitcast.7.temp_hbm, s32[1]{0:T(128)} %bitcast.8.bias_hbm, s32[1,256]{1,0:T(1,128)S(1)} %bitcast.11, bf16[176,256]{1,0:T(8,128)(2,1)} %bitcast.12, bf16[144,256]{1,0:T(8,128)(2,1)} %bitcast.13, bf16[176,1152]{1,0:T(8,128)(2,1)} %wi_hbm.1, ...), custom_call_target="tpu_custom_call" | custom-call | tf_op jit(solution)/shard_map/pair_loss_grads/pallas_call | solution.py:560
  86.3 0.6 copy.13
  86.9 0.6 copy.14
Async XLA Ops:
  1.9 0.7 copy-start

commit v7 on v6

--- a/solution.py
+++ b/solution.py
@@ -113,7 +113,7 @@
         return device(lax.div(k, ZS), lax.rem(k, ZS), c, t)
 
     def tensor_peer(j):
-        dy, dx = ((1, 2), (0, 2), (1, 1), (1, 3), (0, 1), (0, 3), (1, 0))[j - 1]
+        dy, dx = ((1, 2), (0, 2), (1, 0), (1, 1), (1, 3), (0, 1), (0, 3))[j - 1]
         return lax.rem(yhi + dy, 2) * XS + lax.rem(x + dx, XS)
 
     def tensor_steps(body, carry):
@@ -159,12 +159,17 @@
         return lax.dot_general(
             feat[...], weight[...], (((0,), (0,)), ((), ())), preferred_element_type=f32
         ).reshape(TS, R, E)
+
+    def a_encode(part, wire_out):
+        for b in range(2):
+            put(wire_out, b * XS, part[b * XS:(b + 1) * XS].reshape(XS * R, E), R)
 
     g_i[...] = jnp.zeros_like(g_i)
     g_t[...] = jnp.zeros_like(g_t)
     loads[0].wait()
     loads[1].wait()
     part_t[...] = product(ft_ref, wt_ref)
+    a_encode(part_t, a_t_out)
     loads[4].wait()
     pair_out[...] = jnp.broadcast_to(pair_out[0:1, :], (8, 256))
     pl.semaphore_wait(barrier, (TS - 1) + (PS - 1) + 2)
@@ -172,11 +177,11 @@
     def a_copy(wire_out, wire_in, ss, rs, k, slot):
         return copy(wire_out.at[k], wire_in.at[slot], ss.at[k], rs.at[slot], (dp, k))
 
-    def a_send(part, wire_out, wire_in, ss, rs):
-        for hi in (1 - yhi, yhi):
-            put(wire_out, hi * XS, part[pl.ds(hi * XS, XS)].reshape(XS * R, E), R)
-            for d in (2, 1, 3) if hi is yhi else (2, 1, 3, 0):
-                a_copy(wire_out, wire_in, ss, rs, hi * XS + lax.rem(x + d, XS), t).start()
+    def a_send(wire_out, wire_in, ss, rs):
+        def step(j, _):
+            a_copy(wire_out, wire_in, ss, rs, tensor_peer(j), t).start()
+            return 0
+        tensor_steps(step, 0)
 
     def a_take(part, wire_out, wire_in, ss, rs):
         def step(j, total):
@@ -185,13 +190,14 @@
             return total + take(wire_in, k, R)
         return tensor_steps(step, part[t])
 
-    a_send(part_t, a_t_out, a_t_in, a_t_ss, a_t_rs)
+    a_send(a_t_out, a_t_in, a_t_ss, a_t_rs)
     pair_copy = copy(pair_out, pair_in, one_ss.at[0], one_rs.at[0], across)
     pair_copy.start()
     loads[2].wait()
     loads[3].wait()
     part_i[...] = product(fi_ref, wi_ref)
-    a_send(part_i, a_i_out, a_i_in, a_i_ss, a_i_rs)
+    a_encode(part_i, a_i_out)
+    a_send(a_i_out, a_i_in, a_i_ss, a_i_rs)
 
     def local_target(pair):
         r = pair & 31

time: 87.7 us -> 86.7 us (0.989)
  Pallas kernels: 83.7 us -> 82.7 us
    pallas_call x1, Pallas kernels: 83.7 us -> 82.7 us  [on_device(): pl.pallas_call(kernel, out_shape=[jax.ShapeDtypeStruct((OUT, DI), f32), j...]
where the time goes in v7:
time: 86.7 us; the launch traced here: 86.6 us
  Pallas kernels  82.7 us (95%)
  between operations  1.94 us (2%)
  local copies, waits for them, and re-layouts  1.91 us (2%)
    pallas_call x1, Pallas kernels, on_device(): pl.pallas_call(kernel, out_shape=[jax.ShapeDtypeStruct((OUT, DI), f32), j...  82.7 us
    unnamed x4, local copies, waits for them, and re-layouts  1.91 us

profile of v7, /device:TPU:1, one launch (start us, length us, event | category | flops | bytes accessed | tf_op | source)
XLA Modules:
  0.0 86.6 jit_solution(4808071411144464098)
XLA Ops:
  1.9 0.0 copy-start
  1.9 0.7 copy-done
  2.6 82.7 %pair_loss_grads.1 = (f32[36,176]{1,0:T(8,128)S(1)}, f32[36,144]{1,0:T(8,128)S(1)}) custom-call(s32[1]{0:T(128)} %bitcast.7.temp_hbm, s32[1]{0:T(128)} %bitcast.8.bias_hbm, s32[1,256]{1,0:T(1,128)S(1)} %bitcast.11, bf16[176,256]{1,0:T(8,128)(2,1)} %bitcast.12, bf16[144,256]{1,0:T(8,128)(2,1)} %bitcast.13, bf16[176,1152]{1,0:T(8,128)(2,1)} %wi_hbm.1, ...), custom_call_target="tpu_custom_call" | custom-call | tf_op jit(solution)/shard_map/pair_loss_grads/pallas_call | solution.py:566
  85.3 0.6 copy.13
  86.0 0.6 copy.14
Async XLA Ops:
  1.9 0.7 copy-start

commit v8 on v7

--- a/solution.py
+++ b/solution.py
@@ -121,16 +121,19 @@
             carry = body(j, carry)
         return carry
 
-    def z_step(n):
-        m = lax.div(n + 1, 2)
-        return lax.rem(4 + m * (1 - 2 * lax.rem(n, 2)) + ZS, ZS)
+    z_order = (4, 3, 5, 2, 6, 1, 7, 0)
 
     def z_peer(j):
-        return lax.rem(z + z_step(j - 1), ZS)
+        return lax.rem(z + z_order[j - 1], ZS)
 
     def column_peer(j):
         n = j - 1
-        return lax.rem(ylo + 1 - lax.rem(n, 2), 2) * ZS + lax.rem(z + z_step(lax.div(n, 2)), ZS)
+        return lax.rem(ylo + 1 - n % 2, 2) * ZS + lax.rem(z + z_order[n // 2], ZS)
+
+    def unrolled(count, body, carry):
+        for j in range(1, count):
+            carry = body(j, carry)
+        return carry
 
     def copy(src, dst, ssem, rsem, dev):
         return pltpu.make_async_remote_copy(
@@ -151,7 +154,7 @@
         return 0
 
     tensor_steps(greet_tensor, 0)
-    lax.fori_loop(1, PS, greet_column, 0)
+    unrolled(PS, greet_column, 0)
     greet(beyond)
     greet(sibling)
 
@@ -236,7 +239,7 @@
         b_t_copy(z_peer(j), z).start()
         return 0
 
-    lax.fori_loop(1, ZS, b_t_send, 0)
+    unrolled(ZS, b_t_send, 0)
     relay(c, z).start()
 
     halves = ((unit_0, at_x, x, at_y, y), (unit_1, at_y, y, at_x, x))
@@ -281,7 +284,7 @@
         relay(c, zz).start()
         return 0
 
-    lax.fori_loop(1, ZS, b_t_take, 0)
+    unrolled(ZS, b_t_take, 0)
 
     def relay_take(zz, _):
         relay(oc, zz).wait_recv()
@@ -434,7 +437,7 @@
     total = jnp.concatenate([c_i_take(0), c_i_take(1)], axis=0)
     grad_i[t] = back_rows(dir_i[...], norm_i[...], total)
     d_send(grad_i, d_i_ss, d_i_rs)
-    total = lax.fori_loop(1, ZS, c_t_take, gt[c * ZS + z])
+    total = unrolled(ZS, c_t_take, gt[c * ZS + z])
     grad_t[t] = back_rows(dir_t[...], norm_t[...], total)
     d_send(grad_t, d_t_ss, d_t_rs)
 
@@ -459,14 +462,14 @@
             out[k] = (packed[c, k] + sib[k]).astype(bf16)
             e_copy(out, into, ss, rs, k, q).start()
             return 0
-        lax.fori_loop(1, PS, step, 0)
+        unrolled(PS, step, 0)
 
     def e_take(packed, sib, out, into, ss, rs):
         def step(j, total):
             k = column_peer(j)
             e_copy(out, into, ss, rs, k, k).wait_recv()
             return total + into[k].astype(f32)
-        return lax.fori_loop(1, PS, step, packed[c, q] + sib[q])
+        return unrolled(PS, step, packed[c, q] + sib[q])
 
     e_i = (g_i, sib_i, e_i_out, e_i_in, e_i_ss, e_i_rs)
     e_t = (g_t, sib_t, e_t_out, e_t_in, e_t_ss, e_t_rs)
@@ -510,7 +513,7 @@
         return 0
 
     tensor_steps(sent_tensor, 0)
-    lax.fori_loop(1, ZS, sent_z, 0)
+    unrolled(ZS, sent_z, 0)
     lax.fori_loop(0, ZS, sent_relay, 0)
     for d, h in steps:
         me, line = halves[h][2], halves[h][4]
@@ -535,7 +538,7 @@
         e_copy(e_t_out, e_t_in, e_t_ss, e_t_rs, k, q).wait_send()
         return 0
 
-    lax.fori_loop(1, PS, sent_column, 0)
+    unrolled(PS, sent_column, 0)
     for sent in (g_i_copy, g_t_copy):
         sent.wait_send()
 

time: 86.7 us -> 86.5 us (level)
  no operation moved by 1% of the time
where the time goes in v8:
time: 86.5 us; the launch traced here: 86 us
  Pallas kernels  82.2 us (95%)
  between operations  1.94 us (2%)
  local copies, waits for them, and re-layouts  1.91 us (2%)
    pallas_call x1, Pallas kernels, on_device(): pl.pallas_call(kernel, out_shape=[jax.ShapeDtypeStruct((OUT, DI), f32), j...  82.2 us
    unnamed x4, local copies, waits for them, and re-layouts  1.91 us

profile of v8, /device:TPU:1, one launch (start us, length us, event | category | flops | bytes accessed | tf_op | source)
XLA Modules:
  0.0 86.0 jit_solution(5219924436183936597)
XLA Ops:
  1.9 0.0 copy-start
  1.9 0.7 copy-done
  2.6 82.2 %pair_loss_grads.1 = (f32[36,176]{1,0:T(8,128)S(1)}, f32[36,144]{1,0:T(8,128)S(1)}) custom-call(s32[1]{0:T(128)} %bitcast.7.temp_hbm, s32[1]{0:T(128)} %bitcast.8.bias_hbm, s32[1,256]{1,0:T(1,128)S(1)} %bitcast.11, bf16[176,256]{1,0:T(8,128)(2,1)} %bitcast.12, bf16[144,256]{1,0:T(8,128)(2,1)} %bitcast.13, bf16[176,1152]{1,0:T(8,128)(2,1)} %wi_hbm.1, ...), custom_call_target="tpu_custom_call" | custom-call | tf_op jit(solution)/shard_map/pair_loss_grads/pallas_call | solution.py:569
  84.8 0.6 copy.13
  85.4 0.6 copy.14
Async XLA Ops:
  1.9 0.7 copy-start
